TPU v7x, 512 devices: a whole 4x4x16 slice. The times are simulated.
512 devices in a mesh: seq: 4 (over y), mp: 32 (over z, core), cache: 4 (over x).
Axes of the slice: x: 4, y: 4, z: 16, core: 2. Of those that a mesh axis runs over, the one named last changes fastest.
Arguments:
- queries: bfloat16 [4, 1024, 8192], P('cache', 'seq', 'mp'), may hold values from -7 to 7
- span_kv: bfloat16 [4, 1024, 8, 256], P('cache', 'seq'), may hold values from -4 to 4
- pool_kv: bfloat16 [2048, 16, 8, 256], P(('mp', 'cache')), may hold values from -4 to 4
- page_owner: int32 [4, 416, 1], replicated, may hold values from 0 to 127; in each aligned block of 104 rows (0 to 103, 104 to 207, ..., all dimensions but the last counted through in order) at most 2 rows name the same one
- page_slot: int32 [4, 416], replicated, may hold values from 0 to 15
- prefix_len: int32 [4], replicated, may hold values from 1 to 6656, 16640 in all
- ssm_input: bfloat16 [4, 1024, 16384], P('cache', 'seq', 'mp'), may hold values from -6 to 6
- gate_z: bfloat16 [4, 1024, 16384], P('cache', 'seq', 'mp'), may hold values from -6 to 6
- time_step: float32 [4, 1024, 16384], P('cache', 'seq', 'mp'), may hold values from 0 to 0.5, as said below
- bc_weight: bfloat16 [16384, 32], P('mp'), may hold values from -0.046875 to 0.046875
- decay_rate: float32 [16384, 16], P('mp'), may hold values from 0.5 to 2
- skip_gain: float32 [16384], P('mp'), may hold values from 0.5 to 1.5
- state_pool: float32 [16, 16384, 16], P('cache', 'mp'), may hold values from -5 to 5
- state_owner: int32 [4], replicated, may hold values from 0 to 3
- state_slot: int32 [4], replicated, may hold values from 0 to 3
Outputs:
- attn_out: float32 [4, 1024, 8192], P('cache', 'seq', 'mp')
- ssm_out: float32 [4, 1024, 16384], P('cache', 'seq', 'mp')
Inputs may be any that keep to these rules, and one draw needn't show every extreme that they name: `page_owner`: owners are numbered mp index * 4 + cache index. Among the 104 pages of one request and one sequence group (aligned blocks of rows) no owner appears more than 2 times. `time_step`: Positive.
All inputs are finite; a program needn't handle non-finite values.
Results may differ from a plain program's by a relative error of at most 0.0055.
Values may be sent and summed in bfloat16 or wider, within the bound.
No kernel may reach another device: no remote copies, remote signals or barrier semaphores. Data moves between devices by JAX's collectives and lax.ppermute only.
A program may use at most 64 MiB of HBM per device.

v0:
```python
import math

import jax
import jax.numpy as jnp
from jax import lax
from jax.sharding import PartitionSpec as P

big_pos = 1 << 30


def passed_along(value, axis, steps):
    count = lax.axis_size(axis)
    pairs = [(source, (source + steps) % count) for source in range(count)]
    return lax.ppermute(value, axis, pairs)


def carried_in(shard, axis, combine, identity):
    size, index = (lax.axis_size(axis), lax.axis_index(axis))
    everything = jax.tree.map(lambda part: lax.all_gather(part, axis), shard)
    start = jax.tree.map(
        lambda part, zero: jnp.broadcast_to(jnp.asarray(zero, part.dtype), part.shape),
        shard,
        identity,
    )

    def lap(k, before):
        reached = k < index
        new = combine(before, jax.tree.map(lambda part: part[k], everything))
        return jax.tree.map(lambda a, b: jnp.where(reached, a, b), new, before)

    return lax.fori_loop(0, size, lap, start)


def attend_block(carried, query_tile, key_tile, key_pos, query_pos, score_scale):
    running_max, running_sum, running_out = carried
    head_width = query_tile.shape[-1]
    scores = (
        jnp.einsum(
            "tkgd,nkd->kgtn",
            query_tile,
            key_tile[:, :, :head_width],
            preferred_element_type=jnp.float32,
        )
        * score_scale
    )
    allowed = (key_pos[None, :] <= query_pos[:, None])[None, None]
    scores = jnp.where(allowed, scores, -1e30)
    new_max = jnp.maximum(running_max, jnp.max(scores, axis=-1))
    weights = jnp.where(allowed, jnp.exp(scores - new_max[..., None]), 0.0)
    factor = jnp.exp(running_max - new_max)
    running_sum = running_sum * factor + jnp.sum(weights, axis=-1)
    mixed = jnp.einsum(
        "kgtn,nkd->kgtd",
        weights.astype(jnp.bfloat16),
        key_tile[:, :, head_width:],
        preferred_element_type=jnp.float32,
    )
    running_out = running_out * factor[..., None] + mixed
    return (new_max, running_sum, running_out)


def attend(carried, query_tile, key_tile, key_pos, query_pos, score_scale):
    key_count = key_tile.shape[0]
    block_size = math.gcd(key_count, 1024)
    if block_size == key_count:
        return attend_block(carried, query_tile, key_tile, key_pos, query_pos, score_scale)

    def attend_one_block(state_now, pieces):
        return (
            attend_block(state_now, query_tile, pieces[0], pieces[1], query_pos, score_scale),
            None,
        )

    blocks = (
        key_tile.reshape((key_count // block_size, block_size) + key_tile.shape[1:]),
        key_pos.reshape(key_count // block_size, block_size),
    )
    carried, _ = lax.scan(attend_one_block, carried, blocks)
    return carried


def pack_pages(page_owner, page_slot, pool_kv, quarters, slot_cap, kv_dev, local_heads, head_group):
    n_mp = lax.axis_size("mp")
    n_cache = lax.axis_size("cache")
    n_seq = lax.axis_size("seq")
    self_index = lax.axis_index("mp") * n_cache + lax.axis_index("cache")
    pages_dev = page_owner.shape[1] // n_seq
    owners = page_owner[:, :, 0].reshape(n_cache, n_seq, pages_dev)
    slot_ids = page_slot.reshape(n_cache, n_seq, pages_dev)
    is_mine = (owners == self_index).astype(jnp.int32)
    order_rank = jnp.cumsum(is_mine, axis=2) - 1
    places = jnp.arange(slot_cap, dtype=jnp.int32)
    is_hit = (is_mine[..., None] == 1) & (order_rank[..., None] == places)
    chosen = jnp.sum(jnp.where(is_hit, slot_ids[..., None], 0), axis=2).reshape(
        n_cache, quarters * slot_cap
    )
    first_heads = jnp.arange(n_mp, dtype=jnp.int32) * local_heads // head_group
    head_ids = first_heads[:, None] + jnp.arange(kv_dev, dtype=jnp.int32)[None, :]
    row_index = jnp.tile(chosen, (n_mp, 1))
    head_index = jnp.repeat(head_ids, n_cache, axis=0)
    page_lines = jnp.arange(pool_kv.shape[1], dtype=jnp.int32)
    return pool_kv[
        row_index[:, :, None, None], page_lines[None, None, :, None], head_index[:, None, None, :]
    ]


def page_order(page_owner, prefix_len, quarters, slot_cap, page_len):
    n_cache = lax.axis_size("cache")
    n_seq = lax.axis_size("seq")
    owners_total = lax.axis_size("mp") * n_cache
    request_index = lax.axis_index("cache")
    pages_dev = page_owner.shape[1] // n_seq
    owner_row = lax.dynamic_index_in_dim(
        page_owner[:, :, 0], request_index, 0, keepdims=False
    ).reshape(n_seq, pages_dev)
    labels = jnp.arange(owners_total, dtype=jnp.int32)
    owner_match = (owner_row[..., None] == labels).astype(jnp.int32)
    order_rank = jnp.sum(jnp.cumsum(owner_match, axis=1) * owner_match, axis=2) - 1
    quarter_ids = jnp.arange(quarters, dtype=jnp.int32)[:, None]
    target = owner_row * (quarters * slot_cap) + quarter_ids * slot_cap + order_rank
    page_index = quarter_ids * pages_dev + jnp.arange(pages_dev, dtype=jnp.int32)[None, :]
    tokens = page_index.reshape(-1, 1) * page_len + jnp.arange(page_len, dtype=jnp.int32)[None, :]
    length_limit = prefix_len[request_index]
    positions = jnp.where(tokens < length_limit, -1, big_pos).reshape(-1).astype(jnp.int32)
    return (target.reshape(-1), positions)


def ssm_blocks(start_state, step_sizes, drive_term, b_part, c_part, decay_rate, want_out):
    tok_rows, channels = step_sizes.shape
    block_size = math.gcd(tok_rows, 32)
    block_count = tok_rows // block_size

    def ssm_one_block(carried, pieces):
        step_block, drive_block, b_block, c_block = pieces
        climb_rate = jnp.cumsum(step_block, axis=0)[:, :, None] * decay_rate[None]
        pushed = jnp.exp(climb_rate) * drive_block[:, :, None] * b_block[:, None, :]
        states = jnp.exp(-climb_rate) * (carried[None] + jnp.cumsum(pushed, axis=0))
        if want_out:
            result = jnp.sum(states * c_block[:, None, :], axis=2)
        else:
            result = None
        return (states[-1], result)

    pieces = (
        step_sizes.reshape(block_count, block_size, channels),
        drive_term.reshape(block_count, block_size, channels),
        b_part.reshape(block_count, block_size, -1),
        c_part.reshape(block_count, block_size, -1),
    )
    end_state, outputs = lax.scan(ssm_one_block, start_state, pieces)
    if want_out:
        return (end_state, outputs.reshape(tok_rows, channels))
    return (end_state, None)


def chain_link(earlier, later):
    return (earlier[0] * later[0], later[0] * earlier[1] + later[1])


def on_device(
    queries,
    span_kv,
    pool_kv,
    page_owner,
    page_slot,
    prefix_len,
    ssm_input,
    gate_z,
    time_step,
    bc_weight,
    decay_rate,
    skip_gain,
    state_pool,
    state_owner,
    state_slot,
):
    tok_rows = queries.shape[1]
    head_width = span_kv.shape[3] // 2
    kv_heads = span_kv.shape[2]
    local_heads = queries.shape[2] // head_width
    head_group = local_heads * lax.axis_size("mp") // kv_heads
    kv_dev = max(1, local_heads // head_group)
    first_head = lax.axis_index("mp") * local_heads // head_group
    page_len = pool_kv.shape[1]
    n_seq = lax.axis_size("seq")
    seq_index = lax.axis_index("seq")
    pages_dev = page_owner.shape[1] // n_seq
    owners_total = lax.axis_size("mp") * lax.axis_size("cache")
    slot_cap = max(2, (2 * pages_dev + owners_total - 1) // owners_total)
    score_scale = 1.0 / math.sqrt(head_width)
    query_tile = queries[0].reshape(tok_rows, kv_dev, local_heads // kv_dev, head_width)
    query_pos = seq_index * tok_rows + jnp.arange(tok_rows, dtype=jnp.int32)
    span_tile = lax.dynamic_slice_in_dim(span_kv[0], first_head, kv_dev, 1)
    carried = (
        jnp.full((kv_dev, local_heads // kv_dev, tok_rows), -1e30, jnp.float32),
        jnp.zeros((kv_dev, local_heads // kv_dev, tok_rows), jnp.float32),
        jnp.zeros((kv_dev, local_heads // kv_dev, tok_rows, head_width), jnp.float32),
    )
    outgoing = pack_pages(
        page_owner, page_slot, pool_kv, n_seq, slot_cap, kv_dev, local_heads, head_group
    )
    received = lax.all_to_all(outgoing, ("mp", "cache"), split_axis=0, concat_axis=0, tiled=True)
    slot_rows, prefix_pos = page_order(page_owner, prefix_len, n_seq, slot_cap, page_len)
    prefix_keys = received.reshape(-1, page_len, kv_dev, 2 * head_width)[slot_rows].reshape(
        -1, kv_dev, 2 * head_width
    )
    carried = attend(carried, query_tile, prefix_keys, prefix_pos, query_pos, score_scale)
    carried = attend(carried, query_tile, span_tile, query_pos, query_pos, score_scale)
    moving = (span_tile, query_pos)
    for turn_index in range(n_seq - 1):
        moving = passed_along((moving[0], moving[1]), "seq", 1)
        carried = attend(carried, query_tile, moving[0], moving[1], query_pos, score_scale)
    running_max, running_sum, running_out = carried
    attention = running_out / running_sum[..., None]
    attn_out = attention.transpose(2, 0, 1, 3).reshape(tok_rows, local_heads * head_width)[None]
    inputs = ssm_input[0]
    input_values = inputs.astype(jnp.float32)
    step_sizes = time_step[0]
    n_state = decay_rate.shape[1]
    bc_part = jnp.dot(inputs, bc_weight, preferred_element_type=jnp.float32)
    bc_total = lax.psum(bc_part, "mp")
    b_part = bc_total[:, :n_state]
    c_part = bc_total[:, n_state:]
    request_index = lax.axis_index("cache")
    is_owner = state_owner == request_index
    outgoing_states = jnp.where(is_owner[:, None, None], state_pool[state_slot], 0.0)
    incoming_states = lax.all_to_all(
        outgoing_states, "cache", split_axis=0, concat_axis=0, tiled=True
    )
    start_state = lax.dynamic_index_in_dim(
        incoming_states, state_owner[request_index], 0, keepdims=False
    )
    drive_term = step_sizes * input_values
    carry_decay = jnp.exp(-jnp.sum(step_sizes, axis=0)[:, None] * decay_rate)
    local_end, _ = ssm_blocks(
        jnp.zeros_like(start_state), step_sizes, drive_term, b_part, c_part, decay_rate, False
    )
    identity = (jnp.ones_like(carry_decay), jnp.zeros_like(local_end))
    before_decay, before_state = carried_in((carry_decay, local_end), "seq", chain_link, identity)
    entry_state = before_decay * start_state + before_state
    _, read_out = ssm_blocks(entry_state, step_sizes, drive_term, b_part, c_part, decay_rate, True)
    read_out = read_out + skip_gain[None, :] * input_values
    ssm_out = (read_out * jax.nn.silu(gate_z[0].astype(jnp.float32))).astype(jnp.float32)[None]
    return (attn_out, ssm_out)


def solution(mesh):
    in_specs = (
        P("cache", "seq", "mp"),
        P("cache", "seq", None, None),
        P(("mp", "cache"), None, None, None),
        P(),
        P(),
        P(),
        P("cache", "seq", "mp"),
        P("cache", "seq", "mp"),
        P("cache", "seq", "mp"),
        P("mp", None),
        P("mp", None),
        P("mp"),
        P("cache", "mp", None),
        P(),
        P(),
    )
    out_specs = (P("cache", "seq", "mp"), P("cache", "seq", "mp"))
    return jax.shard_map(
        on_device, mesh=mesh, in_specs=in_specs, out_specs=out_specs, check_vma=False
    )
```

profile of v0, /device:TPU:1, one launch (start us, length us, event | category | flops | bytes accessed | tf_op | source)
XLA Modules:
  0.0 802.7 jit_solution(8286018215598789392)
XLA Ops:
  4.3 4.8 all-to-all-start.1
  13.1 175.3 %gather_fusion = bf16[16384,256]{1,0:T(8,128)(2,1)} fusion(bf16[16,16,8,256]{3,2,1,0:T(8,128)(2,1)S(1)} %copy-done, s32[16384]{0:T(1024)S(1)} %reshape.531), kind=kCustom, calls=%fused_computation | custom fusion | bytes 16973824 | tf_op jit(solution)/shard_map/gather | solution.py:102
  189.1 21.0 %all-to-all-start = ((bf16[128,8,16,1,256]{4,2,1,3,0:T(8,128)(2,1)}), bf16[128,8,16,1,256]{4,2,1,3,0:T(8,128)(2,1)}, u32[]{:S(2)}, u32[]{:S(2)}) async-start(bf16[128,8,16,1,256]{4,2,1,3,0:T(8,128)(2,1)} %bitcast.341), calls=%async_computation | async-start | bytes 16777216 | tf_op jit(solution)/shard_map/all_to_all | solution.py:202
  212.2 3.2 collective-permute-start.1
  215.4 3.2 collective-permute-start
  220.4 431.0 %psum.7 = f32[256,32]{0,1:T(8,128)S(1)} all-reduce(f32[256,32]{0,1:T(8,128)S(1)} %fusion.74), channel_id=1, replica_groups=mesh['seq'=4,'mp'=32,'cache'=4] {'mp'}, use_global_device_ids=true, to_apply=%region_17.18 | all-reduce | flops 8192 | bytes 65536 | tf_op jit(solution)/shard_map/psum | solution.py:221
  651.7 4.3 while.53
  656.0 9.6 %all-gather.1 = f32[2048,16]{0,1:T(8,128)S(1)} all-gather(f32[512,16]{0,1:T(8,128)S(1)} %get-tuple-element.233), channel_id=3, replica_groups=mesh['seq'=4,'mp'=32,'cache'=4] {'seq'}, dimensions={0}, use_global_device_ids=true | all-gather | bytes 163840 | tf_op jit(solution)/shard_map/all_gather | solution.py:19
  665.7 9.2 %all-gather = f32[2048,16]{0,1:T(8,128)S(1)} all-gather(f32[512,16]{0,1:T(8,128)S(1)} %multiply_exponential_fusion.1), channel_id=2, replica_groups=mesh['seq'=4,'mp'=32,'cache'=4] {'seq'}, dimensions={0}, use_global_device_ids=true | all-gather | bytes 163840 | tf_op jit(solution)/shard_map/all_gather | solution.py:19
  677.3 2.8 collective-permute-start.2
  680.1 2.7 collective-permute-done.2
  692.8 16.6 %while.54 = (s32[]{:T(128)}, f32[512,16]{0,1:T(8,128)S(1)}, f32[8,32,512]{2,1,0:T(8,128)}, f32[8,32,512]{2,1,0:T(8,128)S(1)}, f32[512,16]{0,1:T(8,128)S(1)}, /*i...) while((s32[]{:T(128)}, f32[512,16]{0,1:T(8,128)S(1)}, ...), condition=%wide.region_28.29_spmd, body=%wide.region_24.28_spmd.sunk | while | flops 10977282 | bytes 1913457 | solution.py:150
  709.5 2.1 fusion.57
  713.5 2.0 fusion.122
  715.5 3.2 collective-permute-done.3
  718.7 2.1 collective-permute-start.5
  722.8 2.9 collective-permute-done.5
  726.3 2.0 fusion.120
  728.3 6.6 gather_fusion.1
  734.9 58.2 %while.55 = (s32[]{:T(128)}, f32[1,2,256]{2,1,0:T(2,128)S(1)}, f32[1,2,256]{2,1,0:T(2,128)S(1)}, f32[1,2,256,128]{3,2,1,0:T(8,128)}, s32[13,512]{1,0:T(8,128)}, ...) while((s32[]{:T(128)}, f32[1,2,256]{2,1,0:T(2,128)S(1)}, ...), condition=%wide.region_7.8_spmd.clone, body=%wide.region_4.7_spmd.clone.sunk | while | flops 136908032 | bytes 5152893 | solution.py:78
  740.7 2.1 fusion.141
  745.3 2.1 fusion.141
  749.8 2.1 fusion.141
  754.4 2.1 fusion.141
  758.9 2.1 fusion.141
  763.4 2.1 fusion.141
  768.0 2.1 fusion.141
  772.5 2.1 fusion.141
  777.1 2.1 fusion.141
  781.6 2.1 fusion.141
  786.2 2.1 fusion.141
  790.7 2.1 fusion.141
  (356 shorter events, 90.3 us)
Async XLA Ops:
  0.6 12.5 %copy-start = (bf16[16,16,8,256]{3,2,1,0:T(8,128)(2,1)S(1)}, bf16[16,16,8,256]{3,2,1,0:T(8,128)(2,1)}, u32[]{:S(2)}) copy-start(bf16[16,16,8,256]{3,2,1,0:T(8,128)(2,1)} %param.25) | copy-start | bytes 3145732
  4.3 184.1 %all-to-all-start.1 = ((f32[4,512,16]{1,2,0:T(8,128)}), f32[4,512,16]{1,2,0:T(8,128)S(1)}, u32[]{:S(2)}, u32[]{:S(2)}) async-start(f32[4,512,16]{1,2,0:T(8,128)} %broadcast_select_fusion.1), calls=%async_computation.1 | async-start | bytes 262144 | tf_op jit(solution)/shard_map/all_to_all | solution.py:227
  188.4 0.6 copy-start.6
  189.0 29.6 %copy-start.10 = (s32[4,416,1]{1,2,0:T(1,128)S(1)}, s32[4,416,1]{1,2,0:T(1,128)}, u32[]{:S(2)}) copy-start(s32[4,416,1]{1,2,0:T(1,128)} %param.26) | copy-start | bytes 19972
  189.0 30.1 %copy-start.13 = (s32[4]{0:T(128)S(1)}, s32[4]{0:T(128)}, u32[]{:S(2)}) copy-start(s32[4]{0:T(128)} %param.28) | copy-start | bytes 52
  189.0 31.2 %copy-start.3 = (bf16[1,256,512]{2,1,0:T(8,128)(2,1)S(1)}, bf16[1,256,512]{2,1,0:T(8,128)(2,1)}, u32[]{:S(2)}) copy-start(bf16[1,256,512]{2,1,0:T(8,128)(2,1)} %param.29) | copy-start | bytes 786436
  189.0 31.2 %copy-start.9 = (bf16[512,32]{0,1:T(8,128)(2,1)S(1)}, bf16[512,32]{0,1:T(8,128)(2,1)}, u32[]{:S(2)}) copy-start(bf16[512,32]{0,1:T(8,128)(2,1)} %param.32) | copy-start | bytes 98308
  189.1 462.4 %copy-start.2 = (f32[1,256,512]{2,1,0:T(8,128)S(1)}, f32[1,256,512]{2,1,0:T(8,128)}, u32[]{:S(2)}) copy-start(f32[1,256,512]{2,1,0:T(8,128)} %param.31) | copy-start | bytes 1572868
  189.1 462.6 %copy-start.1 = (f32[512,16]{0,1:T(8,128)S(1)}, f32[512,16]{0,1:T(8,128)}, u32[]{:S(2)}) copy-start(f32[512,16]{0,1:T(8,128)} %param.33) | copy-start | bytes 98308
  189.1 539.2 %all-to-all-start = ((bf16[128,8,16,1,256]{4,2,1,3,0:T(8,128)(2,1)}), bf16[128,8,16,1,256]{4,2,1,3,0:T(8,128)(2,1)}, u32[]{:S(2)}, u32[]{:S(2)}) async-start(bf16[128,8,16,1,256]{4,2,1,3,0:T(8,128)(2,1)} %bitcast.341), calls=%async_computation | async-start | bytes 16777216 | tf_op jit(solution)/shard_map/all_to_all | solution.py:202
  212.2 499.4 %collective-permute-start.1 = (bf16[256,1,256]{2,0,1:T(8,128)(2,1)}, bf16[256,1,256]{2,0,1:T(8,128)(2,1)}, u32[]{:S(2)}, u32[]{:S(2)}) collective-permute-start(bf16[256,1,256]{2,0,1:T(8,128)(2,1)} %bitcast.301), channel_id=1, source_target_pairs={{0,128},{128,256},{256,384},{384,0},{1,129},{129,257},{257,385},{3... | collective-permute-start | bytes 393224 | tf_op jit(solution)/shard_map/ppermute | solution.py:14
  215.4 461.9 %collective-permute-start = (s32[256]{0:T(256)S(1)}, s32[256]{0:T(256)S(1)}, u32[]{:S(2)}, u32[]{:S(2)}) collective-permute-start(s32[256]{0:T(256)S(1)} %iota_add_fusion.1), channel_id=1, source_target_pairs={{0,128},{128,256},{256,384},{384,0},{1,129},{129,257},{257,385},{3... | collective-permute-start | bytes 3080 | tf_op jit(solution)/shard_map/ppermute | solution.py:14
  651.7 33.1 %copy-start.4 = (bf16[1,256,256]{2,1,0:T(8,128)(2,1)S(1)}, bf16[1,256,256]{2,1,0:T(8,128)(2,1)}, u32[]{:S(2)}) copy-start(bf16[1,256,256]{2,1,0:T(8,128)(2,1)} %param.23) | copy-start | bytes 393220
  651.7 33.9 %copy-start.14 = (s32[4]{0:T(128)S(1)}, s32[4]{0:T(128)}, u32[]{:S(2)}) copy-start(s32[4]{0:T(128)} %param.36) | copy-start | bytes 52
  677.3 12.0 %copy-start.11 = (s32[256]{0:T(256)}, s32[256]{0:T(256)S(1)}, u32[]{:S(2)}) copy-start(s32[256]{0:T(256)S(1)} %collective-permute-done) | copy-start | bytes 3076
  677.3 5.5 collective-permute-start.2
  682.9 6.5 collective-permute-start.4
  692.8 33.5 %copy-start.5 = (pred[256,256]{0,1:T(8,128)(4,1)S(1)}, pred[256,256]{0,1:T(8,128)(4,1)}, u32[]{:S(2)}) copy-start(pred[256,256]{0,1:T(8,128)(4,1)} %get-tuple-element.508) | copy-start | bytes 196612
  709.5 25.5 %copy-start.7 = (bf16[256,1,2,128]{3,0,2,1:T(8,128)(2,1)S(1)}, bf16[256,1,2,128]{3,0,2,1:T(8,128)(2,1)}, u32[]{:S(2)}) copy-start(bf16[256,1,2,128]{3,0,2,1:T(8,128)(2,1)} %copy.119) | copy-start | bytes 393220
  711.6 7.1 collective-permute-start.3
  718.7 2.1 copy-start.8
  718.7 6.9 collective-permute-start.5
  725.6 0.7 copy-start.12
where the time goes:
time: 818 us; the launch traced here: 803 us
  blocking collectives  450 us (55%)
  local copies, waits for them, and re-layouts  229 us (28%)
  matrix products  42.4 us (5%)
  starting transfers between devices  40.9 us (5%)
  other arithmetic  27.9 us (3%)
  waiting for transfers between devices  8.81 us (1%)
    psum x1, blocking collectives, on_device(): bc_total = lax.psum(bc_part, 'mp')  431 us
    gather x1, local copies, waits for them, and re-layouts, pack_pages(): pool_kv[row_index[:, :, None, None], page_lines[None, None, :, None], hea...  175 us
    dot_general x17, matrix products, attend_block(): jnp.einsum('kgtn,nkd->kgtd', weights.astype(jnp.bfloat16), key_tile[:, :,...  31.1 us
    all_to_all x1, starting transfers between devices, on_device(): lax.all_to_all(outgoing, ('mp', 'cache'), split_axis=0, concat_axis=0, ti...  21 us
    all_gather x2, blocking collectives, carried_in(): everything = jax.tree.map(lambda part: lax.all_gather(part, axis), shard)  18.9 us
  transfers between devices with their start and end apart: 8, of which 3 were waited for; matrix products, arithmetic and copies ran while one was open for 27% of the time, Pallas kernels for 0%

commit v1 on v0

v1 whole, which is shorter than its diff:
```python
import functools
import math

import jax
import jax.numpy as jnp
from jax import lax
from jax.experimental import pallas as pl
from jax.experimental.pallas import tpu as pltpu
from jax.sharding import PartitionSpec as P

LOG2E = math.log2(math.e)
HIDDEN = -1e30
FLOOR = -1e29
LANES = 128
STAT_ROWS = 16
MIB = 1 << 20


def params(mib):
    return pltpu.CompilerParams(vmem_limit_bytes=mib * MIB)


def smem():
    return pl.BlockSpec(memory_space=pltpu.SMEM)


def vmem():
    return pl.BlockSpec(memory_space=pltpu.VMEM)


def pack_kernel(chosen_ref, pool_ref, out_ref):
    rows = lax.broadcasted_iota(jnp.int32, (256, 256), 0)
    columns = lax.broadcasted_iota(jnp.int32, (256, 256), 1)
    token, slot, part, head = rows & 3, (rows >> 2) & 1, (rows >> 3) & 3, rows >> 5
    wanted = slot * 128 + (part * 4 + token) * 8 + head
    pick = (columns == wanted).astype(jnp.float32).astype(jnp.bfloat16)
    for request in range(out_ref.shape[0]):
        pages = jnp.concatenate(
            [pool_ref[chosen_ref[2 * request]], pool_ref[chosen_ref[2 * request + 1]]], axis=0
        )
        out_ref[request] = jnp.dot(pick, pages, preferred_element_type=jnp.float32).astype(
            jnp.bfloat16
        )


def compact_kernel(target_ref, received_ref, out_ref):
    count, width = out_ref.shape[0], received_ref.shape[0]
    columns = lax.broadcasted_iota(jnp.int32, (count, width), 1)
    pick = (columns == target_ref[...]).astype(jnp.float32).astype(jnp.bfloat16)
    out_ref[...] = jnp.dot(pick, received_ref[...], preferred_element_type=jnp.float32).astype(
        jnp.bfloat16
    )


def attention_kernel(
    info_ref, query_ref, piece0, piece1, piece2, piece3, span_ref, pos_ref, out_ref, kv_ref
):
    part_rows = piece0.shape[0]
    prefix_rows = 4 * part_rows
    tok_rows = span_ref.shape[0]
    for at, piece in enumerate((piece0, piece1, piece2, piece3)):
        kv_ref[at * part_rows : (at + 1) * part_rows, :] = piece[...]
    kv_ref[prefix_rows:, :] = span_ref[...]
    seq_index, limit = info_ref[0], info_ref[1]
    bias = jnp.where(pos_ref[...] < limit, 0.0, HIDDEN).astype(jnp.float32)
    scale = LOG2E / math.sqrt(LANES)
    row = lax.broadcasted_iota(jnp.int32, (tok_rows, tok_rows), 0)
    column = lax.broadcasted_iota(jnp.int32, (tok_rows, tok_rows), 1)
    stat_row = lax.broadcasted_iota(jnp.int32, (STAT_ROWS, tok_rows), 0)
    for group in range(query_ref.shape[0]):
        seen = row - column + (group - seq_index) * tok_rows >= 0
        stats = jnp.zeros((STAT_ROWS, tok_rows), jnp.float32)
        for head in range(2):
            lanes = slice(head * LANES, (head + 1) * LANES)
            query = query_ref[group, :, lanes]
            dims = (((1,), (1,)), ((), ()))
            far = lax.dot_general(
                query, kv_ref[:prefix_rows, :LANES], dims, preferred_element_type=jnp.float32
            )
            near = lax.dot_general(
                query, kv_ref[prefix_rows:, :LANES], dims, preferred_element_type=jnp.float32
            )
            far = far * scale + bias
            near = jnp.where(seen, near * scale, HIDDEN)
            top = jnp.maximum(
                jnp.max(far, axis=1, keepdims=True), jnp.max(near, axis=1, keepdims=True)
            )
            top = jnp.maximum(top, FLOOR)
            far = jnp.exp2(far - top)
            near = jnp.exp2(near - top)
            total = jnp.sum(far, axis=1, keepdims=True) + jnp.sum(near, axis=1, keepdims=True)
            total = jnp.maximum(total, 1e-37)
            mixed = jnp.dot(
                far.astype(jnp.bfloat16),
                kv_ref[:prefix_rows, LANES:],
                preferred_element_type=jnp.float32,
            ) + jnp.dot(
                near.astype(jnp.bfloat16),
                kv_ref[prefix_rows:, LANES:],
                preferred_element_type=jnp.float32,
            )
            out_ref[group, :tok_rows, lanes] = (mixed / total).astype(jnp.bfloat16)
            level = top + jnp.log2(total)
            level = jnp.transpose(jnp.broadcast_to(level, (tok_rows, LANES)))[:STAT_ROWS]
            high = level.astype(jnp.bfloat16).astype(jnp.float32)
            middle = (level - high).astype(jnp.bfloat16).astype(jnp.float32)
            low = level - high - middle
            for at, value in enumerate((high, middle, low)):
                stats = jnp.where(stat_row == 3 * head + at, value, stats)
        out_ref[group, tok_rows:, :] = stats.astype(jnp.bfloat16)


def combine_kernel(part_ref, out_ref):
    groups = part_ref.shape[0]
    tok_rows = out_ref.shape[0]
    stats = [part_ref[group, tok_rows:, :].astype(jnp.float32) for group in range(groups)]
    shares = []
    for head in range(2):
        levels = [
            stat[3 * head : 3 * head + 1]
            + stat[3 * head + 1 : 3 * head + 2]
            + stat[3 * head + 2 : 3 * head + 3]
            for stat in stats
        ]
        top = functools.reduce(jnp.maximum, levels)
        weights = [jnp.exp2(level - top) for level in levels]
        total = functools.reduce(jnp.add, weights)
        shares.append([weight / total for weight in weights])
    share_row = lax.broadcasted_iota(jnp.int32, (LANES, tok_rows), 0)
    table = jnp.zeros((LANES, tok_rows), jnp.float32)
    for head in range(2):
        for group in range(groups):
            table = jnp.where(share_row == head * groups + group, shares[head][group], table)
    table = jnp.transpose(table)
    for head in range(2):
        lanes = slice(head * LANES, (head + 1) * LANES)
        mixed = jnp.zeros((tok_rows, LANES), jnp.float32)
        for group in range(groups):
            at = head * groups + group
            mixed = mixed + table[:, at : at + 1] * part_ref[group, :tok_rows, lanes].astype(
                jnp.float32
            )
        out_ref[:, lanes] = mixed


BLOCK = 16


def scan_tokens(step_ref, input_ref, bc_ref, decay, state, read_out):
    tokens = step_ref.shape[0]
    n_state = decay.shape[0]

    for half in range(tokens // LANES):
        bc_half = bc_ref[:, half * LANES : (half + 1) * LANES]

        def block(at, carried, half=half, bc_half=bc_half):
            start = pl.multiple_of(half * LANES + at * BLOCK, BLOCK)
            steps = step_ref[pl.ds(start, BLOCK), :]
            inputs = input_ref[pl.ds(start, BLOCK), :].astype(jnp.float32)
            drive = steps * inputs
            turned = pltpu.roll(bc_half, LANES - at * BLOCK, 1)
            rows = []
            for i in range(BLOCK):
                factor = jnp.exp2(steps[i : i + 1] * decay)
                carried = factor * carried + drive[i : i + 1] * turned[:n_state, i : i + 1]
                if read_out is not None:
                    term = carried * turned[n_state:, i : i + 1]
                    rows.append(jnp.sum(term, axis=0, keepdims=True))
            if read_out is not None:
                read_out(start, inputs, jnp.concatenate(rows, axis=0))
            return carried

        state = lax.fori_loop(0, LANES // BLOCK, block, state)
    return state


def local_scan_kernel(step_ref, input_ref, bc_ref, rate_ref, out_ref):
    decay = rate_ref[...] * (-LOG2E)
    n_state = decay.shape[0]
    out_ref[:n_state] = scan_tokens(
        step_ref, input_ref, bc_ref, decay, jnp.zeros(decay.shape, jnp.float32), None
    )
    total = jnp.sum(step_ref[...], axis=0, keepdims=True)
    out_ref[n_state:] = jnp.broadcast_to(total, (out_ref.shape[0] - n_state, total.shape[1]))


def full_scan_kernel(
    info_ref, step_ref, input_ref, gate_ref, bc_ref, rate_ref, skip_ref, carry_ref, start_ref, out_ref
):
    decay = rate_ref[...] * (-LOG2E)
    n_state = decay.shape[0]
    state = start_ref[...]
    for group in range(carry_ref.shape[0] - 1):
        factor = jnp.exp2(carry_ref[group, n_state : n_state + 1, :] * decay)
        moved = factor * state + carry_ref[group, :n_state, :]
        state = jnp.where(group < info_ref[0], moved, state)
    skip = skip_ref[...]

    def read_out(start, inputs, values):
        gate = gate_ref[pl.ds(start, BLOCK), :].astype(jnp.float32)
        out_ref[pl.ds(start, BLOCK), :] = (values + skip * inputs) * (gate / (1.0 + jnp.exp(-gate)))

    scan_tokens(step_ref, input_ref, bc_ref, decay, state, read_out)


def call(kernel, out, specs, args, mib, scratch=()):
    return pl.pallas_call(
        kernel,
        out_shape=out,
        in_specs=specs,
        out_specs=vmem(),
        scratch_shapes=list(scratch),
        compiler_params=params(mib),
    )(*args)


def shared_with(value, axis, groups=None):
    count = len(groups[0]) if groups else lax.axis_size(axis)
    everything = jnp.broadcast_to(value[None], (count,) + value.shape)
    return lax.all_to_all(
        everything, axis, split_axis=0, concat_axis=0, tiled=True, axis_index_groups=groups
    )


def swapped(value, flip):
    count = lax.axis_size("mp")
    return lax.ppermute(value, "mp", [(source, source ^ flip) for source in range(count)])


def on_device(
    queries,
    span_kv,
    pool_kv,
    page_owner,
    page_slot,
    prefix_len,
    ssm_input,
    gate_z,
    time_step,
    bc_weight,
    decay_rate,
    skip_gain,
    state_pool,
    state_owner,
    state_slot,
):
    n_seq, n_mp, n_cache = (lax.axis_size(axis) for axis in ("seq", "mp", "cache"))
    seq_index, mp_index, request = (lax.axis_index(axis) for axis in ("seq", "mp", "cache"))
    tok_rows = queries.shape[1]
    kv_heads, width = span_kv.shape[2], span_kv.shape[3]
    pool_pages, page_len = pool_kv.shape[:2]
    pages_dev = page_owner.shape[1] // n_seq
    sharers = n_mp // kv_heads
    page_part = page_len // sharers
    head, part = mp_index // sharers, mp_index % sharers

    quarter_owner = lax.dynamic_slice_in_dim(page_owner[:, :, 0], seq_index * pages_dev, pages_dev, 1)
    quarter_slot = lax.dynamic_slice_in_dim(page_slot, seq_index * pages_dev, pages_dev, 1)
    earlier = jnp.tril(jnp.ones((pages_dev, pages_dev), jnp.bool_), -1)
    same = quarter_owner[:, :, None] == quarter_owner[:, None, :]
    rank = jnp.sum((same & earlier).astype(jnp.int32), axis=2)
    mine = quarter_owner == mp_index * n_cache + request
    places = jnp.arange(2, dtype=jnp.int32)
    hit = mine[:, None, :] & (rank[:, None, :] == places[None, :, None])
    chosen = jnp.sum(jnp.where(hit, quarter_slot[:, None, :], 0), axis=2).reshape(-1)

    outgoing = call(
        pack_kernel,
        jax.ShapeDtypeStruct((n_cache, n_mp * 2 * page_part, width), jnp.bfloat16),
        [smem(), vmem()],
        (chosen, pool_kv.reshape(pool_pages, page_len * kv_heads, width)),
        24,
    )
    received = lax.all_to_all(
        outgoing.reshape(n_cache * n_mp, 2 * page_part, width),
        ("cache", "mp"),
        split_axis=0,
        concat_axis=0,
        tiled=True,
    ).reshape(n_cache * n_mp * 2 * page_part, width)

    all_queries = shared_with(queries[0], "seq")

    inputs = ssm_input[0]
    bc = lax.dot_general(
        bc_weight, inputs, (((0,), (1,)), ((), ())), preferred_element_type=jnp.float32
    )
    near = [[base + i for i in range(8)] for base in range(0, n_mp, 8)]
    across = [[base + i for i in range(0, n_mp, 8)] for base in range(8)]
    bc = jnp.sum(shared_with(bc, "mp", near), axis=0)
    bc = jnp.sum(shared_with(bc, "mp", across), axis=0)

    states = state_pool.transpose(0, 2, 1)
    leaving = jnp.where((state_owner == request)[:, None, None], states[state_slot], 0.0)
    arriving = lax.all_to_all(leaving, "cache", split_axis=0, concat_axis=0, tiled=True)
    start_state = lax.dynamic_index_in_dim(arriving, state_owner[request], 0, keepdims=False)

    rate = decay_rate.T
    n_state = rate.shape[0]
    carry = call(
        local_scan_kernel,
        jax.ShapeDtypeStruct((n_state + 8, rate.shape[1]), jnp.float32),
        [vmem()] * 4,
        (time_step[0], inputs, bc, rate),
        24,
    )
    carries = shared_with(carry, "seq")
    ssm_out = call(
        full_scan_kernel,
        jax.ShapeDtypeStruct(inputs.shape, jnp.float32),
        [smem()] + [vmem()] * 8,
        (
            seq_index.reshape(1),
            time_step[0],
            inputs,
            gate_z[0],
            bc,
            rate,
            skip_gain.reshape(1, -1),
            carries,
            start_state,
        ),
        24,
    )

    my_owner = lax.dynamic_index_in_dim(quarter_owner, request, 0, keepdims=False)
    my_rank = lax.dynamic_index_in_dim(rank, request, 0, keepdims=False)
    base = ((my_owner % n_cache) * n_mp + my_owner // n_cache) * (2 * page_part) + my_rank * page_part
    tokens = jnp.arange(page_part, dtype=jnp.int32)
    target = (base[None, :] + tokens[:, None]).reshape(-1, 1)
    page = seq_index * pages_dev + jnp.arange(pages_dev, dtype=jnp.int32)
    in_page = (part ^ jnp.arange(sharers, dtype=jnp.int32))[:, None] * page_part + tokens[None, :]
    position = (page[None, None, :] * page_len + in_page[:, :, None]).reshape(1, -1)

    own = call(
        compact_kernel,
        jax.ShapeDtypeStruct((page_part * pages_dev, width), jnp.bfloat16),
        [vmem()] * 2,
        (target, received),
        24,
    )
    pieces = [own] + [swapped(own, flip) for flip in range(1, sharers)]
    span_tile = lax.dynamic_index_in_dim(span_kv[0], head, 1, keepdims=False)
    partial = call(
        attention_kernel,
        jax.ShapeDtypeStruct((n_seq, tok_rows + STAT_ROWS, queries.shape[2]), jnp.bfloat16),
        [smem()] + [vmem()] * 7,
        (
            jnp.stack([seq_index, prefix_len[request]]).astype(jnp.int32),
            all_queries,
            *pieces,
            span_tile,
            position,
        ),
        40,
        [pltpu.VMEM((sharers * page_part * pages_dev + tok_rows, width), jnp.bfloat16)],
    )
    gathered = lax.all_to_all(partial, "seq", split_axis=0, concat_axis=0, tiled=True)
    attn_out = call(
        combine_kernel,
        jax.ShapeDtypeStruct((tok_rows, queries.shape[2]), jnp.float32),
        [vmem()],
        (gathered,),
        24,
    )
    return (attn_out[None], ssm_out[None])


def solution(mesh):
    in_specs = (
        P("cache", "seq", "mp"),
        P("cache", "seq", None, None),
        P(("mp", "cache"), None, None, None),
        P(),
        P(),
        P(),
        P("cache", "seq", "mp"),
        P("cache", "seq", "mp"),
        P("cache", "seq", "mp"),
        P("mp", None),
        P("mp", None),
        P("mp"),
        P("cache", "mp", None),
        P(),
        P(),
    )
    out_specs = (P("cache", "seq", "mp"), P("cache", "seq", "mp"))
    return jax.shard_map(
        on_device, mesh=mesh, in_specs=in_specs, out_specs=out_specs, check_vma=False
    )
```

time: 818 us -> 149 us (0.18); the launches traced: 803 us -> 148 us
  blocking collectives: 450 us -> 0 us
  local copies, waits for them, and re-layouts: 229 us -> 9.58 us
  waiting for transfers between devices: 8.81 us -> 54.1 us
  matrix products: 42.4 us -> 1.23 us
  other arithmetic: 27.9 us -> 3.53 us
  Pallas kernels: 0 us -> 21.6 us
  starting transfers between devices: 40.9 us -> 54.8 us
    psum x1 -> x0, blocking collectives: 431 us -> none  [on_device(): bc_total = lax.psum(bc_part, 'mp')]
    gather x3 -> x1, local copies, waits for them, and re-layouts: 183 us -> 0.56 us  [on_device(): states[state_slot]]
    all_to_all x2 -> x7, waiting for transfers between devices: 0.01 us -> 53.9 us  [the longest x1 32.1 us: on_device(): lax.all_to_all(outgoing.reshape(n_cache * n_mp, 2 * page_part, width), ('...]
    dot_general x35 -> x1, matrix products: 42.4 us -> 1.23 us  [on_device(): lax.dot_general(bc_weight, inputs, (((0,), (1,)), ((), ())), preferred_el...]
    pallas_call x0 -> x6, Pallas kernels: none -> 21.6 us  [call(): pl.pallas_call(kernel, out_shape=out, in_specs=specs, out_specs=vmem(), s...]
    all_to_all x2 -> x7, starting transfers between devices: 25.8 us -> 45.7 us  [the longest x4 29.3 us: shared_with(): lax.all_to_all(everything, axis, split_axis=0, concat_axis=0, tiled=True,...]
    all_gather x2 -> x0, blocking collectives: 18.9 us -> none  [carried_in(): everything = jax.tree.map(lambda part: lax.all_gather(part, axis), shard)]
    squeeze x21 -> x1, local copies, waits for them, and re-layouts: 12.7 us -> 0.01 us  [on_device(): lax.dynamic_index_in_dim(arriving, state_owner[request], 0, keepdims=False)]
  transfers between devices with their start and end apart: 8 -> 10, of which waited for: 3 -> 6; matrix products, arithmetic and copies ran while one was open for 27% -> 6% of each run, Pallas kernels for 0% -> 14%
where the time goes in v1:
time: 149 us; the launch traced here: 148 us
  starting transfers between devices  54.8 us (37%)
  waiting for transfers between devices  54.1 us (36%)
  Pallas kernels  21.6 us (14%)
  local copies, waits for them, and re-layouts  9.58 us (6%)
  other arithmetic  3.53 us (2%)
  between operations  2.93 us (2%)
    all_to_all x1, waiting for transfers between devices, on_device(): lax.all_to_all(outgoing.reshape(n_cache * n_mp, 2 * page_part, width), ('...  32.1 us
    all_to_all x4, starting transfers between devices, shared_with(): lax.all_to_all(everything, axis, split_axis=0, concat_axis=0, tiled=True,...  29.3 us
    pallas_call x6, Pallas kernels, call(): pl.pallas_call(kernel, out_shape=out, in_specs=specs, out_specs=vmem(), s...  21.6 us
    all_to_all x4, waiting for transfers between devices, shared_with(): lax.all_to_all(everything, axis, split_axis=0, concat_axis=0, tiled=True,...  17.2 us
    ppermute x3, starting transfers between devices, swapped(): lax.ppermute(value, 'mp', [(source, source ^ flip) for source in range(co...  9.02 us
    all_to_all x1, starting transfers between devices, on_device(): lax.all_to_all(outgoing.reshape(n_cache * n_mp, 2 * page_part, width), ('...  8.37 us
    all_to_all x1, starting transfers between devices, on_device(): lax.all_to_all(partial, 'seq', split_axis=0, concat_axis=0, tiled=True)  4.75 us
    all_to_all x1, waiting for transfers between devices, on_device(): lax.all_to_all(leaving, 'cache', split_axis=0, concat_axis=0, tiled=True)  4.53 us
  transfers between devices with their start and end apart: 10, of which 6 were waited for; matrix products, arithmetic and copies ran while one was open for 6% of the time, Pallas kernels for 14%

profile of v1, /device:TPU:1, one launch (start us, length us, event | category | flops | bytes accessed | tf_op | source)
XLA Modules:
  0.0 147.7 jit_solution(8896259991586730034)
XLA Ops:
  0.6 1.2 fusion.7
  1.9 0.7 broadcast_in_dim.47
  2.7 10.3 %all-to-all-start.3 = ((f32[8,32,256]{2,1,0:T(8,128)}), f32[8,32,256]{2,1,0:T(8,128)S(1)}, u32[]{:S(2)}, u32[]{:S(2)}) async-start(f32[8,32,256]{2,1,0:T(8,128)} %broadcast_in_dim.47), calls=%async_computation.3 | async-start | bytes 524288 | tf_op jit(solution)/shard_map/all_to_all | solution.py:220
  13.6 0.8 constant_dynamic-slice_fusion.3
  14.5 0.7 broadcast_select_fusion
  15.2 6.5 %all-to-all-done.3 = f32[8,32,256]{2,1,0:T(8,128)S(1)} async-done(((f32[8,32,256]{2,1,0:T(8,128)}), f32[8,32,256]{2,1,0:T(8,128)S(1)}, u32[]{:S(2)}, u32[]{:S(2)}) %all-to-all-start.3) | async-done | bytes 262176 | tf_op jit(solution)/shard_map/all_to_all | solution.py:220
  21.7 3.3 %all-to-all-start.6 = ((f32[4,16,512]{2,1,0:T(8,128)}), f32[4,16,512]{2,1,0:T(8,128)S(1)}, u32[]{:S(2)}, u32[]{:S(2)}) async-start(f32[4,16,512]{2,1,0:T(8,128)} %broadcast_select_fusion), calls=%async_computation.6 | async-start | bytes 262144 | tf_op jit(solution)/shard_map/all_to_all | solution.py:295
  25.3 4.5 %all-to-all-done.6 = f32[4,16,512]{2,1,0:T(8,128)S(1)} async-done(((f32[4,16,512]{2,1,0:T(8,128)}), f32[4,16,512]{2,1,0:T(8,128)S(1)}, u32[]{:S(2)}, u32[]{:S(2)}) %all-to-all-start.6) | async-done | bytes 131104 | tf_op jit(solution)/shard_map/all_to_all | solution.py:295
  29.8 0.7 broadcast_in_dim.48
  30.5 10.1 %all-to-all-start.4 = ((f32[4,32,256]{2,1,0:T(8,128)}), f32[4,32,256]{2,1,0:T(8,128)S(1)}, u32[]{:S(2)}, u32[]{:S(2)}) async-start(f32[4,32,256]{2,1,0:T(8,128)} %broadcast_in_dim.48), calls=%async_computation.4 | async-start | bytes 262144 | tf_op jit(solution)/shard_map/all_to_all | solution.py:220
  40.6 0.8 constant_dynamic-slice_fusion.1
  41.7 1.7 %shard_map.158 = bf16[4,256,256]{2,1,0:T(8,128)(2,1)} custom-call(s32[8]{0:T(128)S(1)} %reshape.234.chosen_ref, bf16[16,128,256]{2,1,0:T(8,128)(2,1)S(1)} %bitcast.36), custom_call_target="tpu_custom_call" | custom-call | tf_op jit(solution)/shard_map/pallas_call | solution.py:207
  43.4 10.7 %all-to-all-done.4 = f32[4,32,256]{2,1,0:T(8,128)S(1)} async-done(((f32[4,32,256]{2,1,0:T(8,128)}), f32[4,32,256]{2,1,0:T(8,128)S(1)}, u32[]{:S(2)}, u32[]{:S(2)}) %all-to-all-start.4) | async-done | bytes 131104 | tf_op jit(solution)/shard_map/all_to_all | solution.py:220
  54.0 8.4 %all-to-all-start.1 = ((bf16[128,8,256]{2,1,0:T(8,128)(2,1)}), bf16[128,8,256]{2,1,0:T(8,128)(2,1)S(1)}, u32[]{:S(2)}, u32[]{:S(2)}) async-start(bf16[128,8,256]{2,1,0:T(8,128)(2,1)} %bitcast.6), calls=%async_computation.1 | async-start | bytes 1048576 | tf_op jit(solution)/shard_map/all_to_all | solution.py:274
  62.5 0.8 fusion.6
  63.5 32.1 %all-to-all-done.1 = bf16[128,8,256]{2,1,0:T(8,128)(2,1)S(1)} async-done(((bf16[128,8,256]{2,1,0:T(8,128)(2,1)}), bf16[128,8,256]{2,1,0:T(8,128)(2,1)S(1)}, u32[]{:S(2)}, u32[]{:S(2)}) %all-to-all-start.1) | async-done | bytes 524320 | tf_op jit(solution)/shard_map/all_to_all | solution.py:274
  95.6 0.8 broadcast_in_dim.43
  96.5 4.3 %all-to-all-start = ((bf16[4,256,256]{2,1,0:T(8,128)(2,1)}), bf16[4,256,256]{2,1,0:T(8,128)(2,1)S(1)}, u32[]{:S(2)}, u32[]{:S(2)}) async-start(bf16[4,256,256]{2,1,0:T(8,128)(2,1)} %broadcast_in_dim.43), calls=%async_computation | async-start | bytes 1048576 | tf_op jit(solution)/shard_map/all_to_all | solution.py:220
  100.9 0.7 broadcast_add_fusion
  101.6 0.7 copy-done.5
  102.3 3.3 %shard_map.162 = f32[24,512]{1,0:T(8,128)S(1)} custom-call(f32[256,512]{1,0:T(8,128)S(1)} %bitcast.33, bf16[256,512]{1,0:T(8,128)(2,1)S(1)} %bitcast.31, f32[32,256]{1,0:T(8,128)S(1)} %reduce_sum.39.bc_ref, f32[16,512]{1,0:T(8,128)S(1)} %bitcast.39), custom_call_target="tpu_custom_call" | custom-call | tf_op jit(solution)/shard_map/pallas_call | solution.py:207
  106.2 3.4 %collective-permute-start = (bf16[416,256]{1,0:T(8,128)(2,1)S(1)}, bf16[416,256]{1,0:T(8,128)(2,1)S(1)}, u32[]{:S(2)}, u32[]{:S(2)}) collective-permute-start(bf16[416,256]{1,0:T(8,128)(2,1)S(1)} %shard_map.159.piece0), channel_id=1, source_target_pairs={{0,4},{4,0},{8,12},{12,8},{16,20},{20,16},{24,28},{28,24},{32,36},... | collective-permute-start | bytes 638984 | tf_op jit(solution)/shard_map/ppermute | solution.py:227
  109.6 3.7 %collective-permute-start.1 = (bf16[416,256]{1,0:T(8,128)(2,1)S(1)}, bf16[416,256]{1,0:T(8,128)(2,1)}, u32[]{:S(2)}, u32[]{:S(2)}) collective-permute-start(bf16[416,256]{1,0:T(8,128)(2,1)S(1)} %shard_map.159.piece0), channel_id=1, source_target_pairs={{0,8},{4,12},{8,0},{12,4},{16,24},{20,28},{24,16},{28,20},{32,40},... | collective-permute-start | bytes 638984 | tf_op jit(solution)/shard_map/ppermute | solution.py:227
  113.3 1.9 %collective-permute-start.2 = (bf16[416,256]{1,0:T(8,128)(2,1)S(1)}, bf16[416,256]{1,0:T(8,128)(2,1)}, u32[]{:S(2)}, u32[]{:S(2)}) collective-permute-start(bf16[416,256]{1,0:T(8,128)(2,1)S(1)} %shard_map.159.piece0), channel_id=1, source_target_pairs={{0,12},{4,8},{8,4},{12,0},{16,28},{20,24},{24,20},{28,16},{32,44},... | collective-permute-start | bytes 638984 | tf_op jit(solution)/shard_map/ppermute | solution.py:227
  115.2 0.7 broadcast_in_dim.49
  115.9 4.5 %all-to-all-start.5 = ((f32[4,24,512]{2,1,0:T(8,128)}), f32[4,24,512]{2,1,0:T(8,128)S(1)}, u32[]{:S(2)}, u32[]{:S(2)}) async-start(f32[4,24,512]{2,1,0:T(8,128)} %broadcast_in_dim.49), calls=%async_computation.5 | async-start | bytes 393216 | tf_op jit(solution)/shard_map/all_to_all | solution.py:220
  122.6 0.7 pad_add_fusion.info_ref
  123.5 9.0 %shard_map.160 = bf16[4,272,256]{2,1,0:T(8,128)(2,1)} custom-call(s32[2]{0:T(128)S(1)} %pad_add_fusion.info_ref, bf16[4,256,256]{2,1,0:T(8,128)(2,1)S(1)} %all-to-all-done.query_ref, bf16[416,256]{1,0:T(8,128)(2,1)S(1)} %shard_map.159.piece0, bf16[416,256]{1,0:T(8,128)(2,1)S(1)} %collective-permute-done.piece1, ...), custom_call_target="tpu_custom_call" | custom-call | tf_op jit(solution)/shard_map/pallas_call | solution.py:207
  132.5 4.8 %all-to-all-start.2 = ((bf16[4,272,256]{2,1,0:T(8,128)(2,1)}), bf16[4,272,256]{2,1,0:T(8,128)(2,1)S(1)}, u32[]{:S(2)}, u32[]{:S(2)}) async-start(bf16[4,272,256]{2,1,0:T(8,128)(2,1)} %shard_map.160), calls=%async_computation.2 | async-start | bytes 1114112 | tf_op jit(solution)/shard_map/all_to_all | solution.py:358
  139.8 0.7 copy-done.6
  140.5 5.9 %shard_map.163 = f32[256,512]{1,0:T(8,128)} custom-call(s32[1]{0:T(128)} %bitcast.info_ref, f32[256,512]{1,0:T(8,128)S(1)} %bitcast.34, bf16[256,512]{1,0:T(8,128)(2,1)S(1)} %bitcast.32, bf16[256,512]{1,0:T(8,128)(2,1)S(1)} %bitcast.38, f32[32,256]{1,0:T(8,128)S(1)} %reduce_sum.39.bc_ref, f32[16,512]{1,0:T(8,128)S(1)} %bitcast.40, f32[1,512]{1,0:T(1,128)S(1)} %bitcast.41, ...), custom_call_target="tpu_custom_call" | custom-call | tf_op jit(solution)/shard_map/pallas_call | solution.py:207
  146.5 1.3 shard_map.161
  (57 shorter events, 5.2 us)
Async XLA Ops:
  0.6 119.8 %copy-start = (bf16[1,256,8,256]{3,2,1,0:T(8,128)(2,1)S(1)}, bf16[1,256,8,256]{3,2,1,0:T(8,128)(2,1)}, u32[]{:S(2)}) copy-start(bf16[1,256,8,256]{3,2,1,0:T(8,128)(2,1)} %param.16) | copy-start | bytes 3145732
  1.9 11.1 %copy-start.10 = (s32[4]{0:T(128)S(1)}, s32[4]{0:T(128)}, u32[]{:S(2)}) copy-start(s32[4]{0:T(128)} %param.29) | copy-start | bytes 52
  1.9 11.1 %copy-start.8 = (f32[4,512,16]{1,2,0:T(8,128)S(1)}, f32[4,512,16]{1,2,0:T(8,128)}, u32[]{:S(2)}) copy-start(f32[4,512,16]{1,2,0:T(8,128)} %param.27) | copy-start | bytes 393220
  1.9 12.5 %copy-start.12 = (s32[4]{0:T(128)S(1)}, s32[4]{0:T(128)}, u32[]{:S(2)}) copy-start(s32[4]{0:T(128)} %param.28) | copy-start | bytes 52
  2.6 39.1 %copy-start.3 = (bf16[16,16,8,256]{3,2,1,0:T(8,128)(2,1)S(1)}, bf16[16,16,8,256]{3,2,1,0:T(8,128)(2,1)}, u32[]{:S(2)}) copy-start(bf16[16,16,8,256]{3,2,1,0:T(8,128)(2,1)} %param.17) | copy-start | bytes 3145732
  2.7 19.1 %all-to-all-start.3 = ((f32[8,32,256]{2,1,0:T(8,128)}), f32[8,32,256]{2,1,0:T(8,128)S(1)}, u32[]{:S(2)}, u32[]{:S(2)}) async-start(f32[8,32,256]{2,1,0:T(8,128)} %broadcast_in_dim.47), calls=%async_computation.3 | async-start | bytes 524288 | tf_op jit(solution)/shard_map/all_to_all | solution.py:220
  21.7 8.1 %all-to-all-start.6 = ((f32[4,16,512]{2,1,0:T(8,128)}), f32[4,16,512]{2,1,0:T(8,128)S(1)}, u32[]{:S(2)}, u32[]{:S(2)}) async-start(f32[4,16,512]{2,1,0:T(8,128)} %broadcast_select_fusion), calls=%async_computation.6 | async-start | bytes 262144 | tf_op jit(solution)/shard_map/all_to_all | solution.py:295
  30.5 23.6 %all-to-all-start.4 = ((f32[4,32,256]{2,1,0:T(8,128)}), f32[4,32,256]{2,1,0:T(8,128)S(1)}, u32[]{:S(2)}, u32[]{:S(2)}) async-start(f32[4,32,256]{2,1,0:T(8,128)} %broadcast_in_dim.48), calls=%async_computation.4 | async-start | bytes 262144 | tf_op jit(solution)/shard_map/all_to_all | solution.py:220
  54.0 41.6 %all-to-all-start.1 = ((bf16[128,8,256]{2,1,0:T(8,128)(2,1)}), bf16[128,8,256]{2,1,0:T(8,128)(2,1)S(1)}, u32[]{:S(2)}, u32[]{:S(2)}) async-start(bf16[128,8,256]{2,1,0:T(8,128)(2,1)} %bitcast.6), calls=%async_computation.1 | async-start | bytes 1048576 | tf_op jit(solution)/shard_map/all_to_all | solution.py:274
  62.4 33.2 %copy-start.7 = (bf16[1,256,256]{2,1,0:T(8,128)(2,1)S(1)}, bf16[1,256,256]{2,1,0:T(8,128)(2,1)}, u32[]{:S(2)}) copy-start(bf16[1,256,256]{2,1,0:T(8,128)(2,1)} %param.15) | copy-start | bytes 393220
  96.5 5.1 %copy-start.1 = (bf16[1,256,512]{2,1,0:T(8,128)(2,1)S(1)}, bf16[1,256,512]{2,1,0:T(8,128)(2,1)}, u32[]{:S(2)}) copy-start(bf16[1,256,512]{2,1,0:T(8,128)(2,1)} %param.21) | copy-start | bytes 786436
  96.5 5.1 %copy-start.2 = (f32[1,256,512]{2,1,0:T(8,128)S(1)}, f32[1,256,512]{2,1,0:T(8,128)}, u32[]{:S(2)}) copy-start(f32[1,256,512]{2,1,0:T(8,128)} %param.23) | copy-start | bytes 1572868
  96.5 18.7 %all-to-all-start = ((bf16[4,256,256]{2,1,0:T(8,128)(2,1)}), bf16[4,256,256]{2,1,0:T(8,128)(2,1)S(1)}, u32[]{:S(2)}, u32[]{:S(2)}) async-start(bf16[4,256,256]{2,1,0:T(8,128)(2,1)} %broadcast_in_dim.43), calls=%async_computation | async-start | bytes 1048576 | tf_op jit(solution)/shard_map/all_to_all | solution.py:220
  101.5 0.8 copy-start.5
  106.2 17.2 %collective-permute-start = (bf16[416,256]{1,0:T(8,128)(2,1)S(1)}, bf16[416,256]{1,0:T(8,128)(2,1)S(1)}, u32[]{:S(2)}, u32[]{:S(2)}) collective-permute-start(bf16[416,256]{1,0:T(8,128)(2,1)S(1)} %shard_map.159.piece0), channel_id=1, source_target_pairs={{0,4},{4,0},{8,12},{12,8},{16,20},{20,16},{24,28},{28,24},{32,36},... | collective-permute-start | bytes 638984 | tf_op jit(solution)/shard_map/ppermute | solution.py:227
  109.6 13.8 %collective-permute-start.1 = (bf16[416,256]{1,0:T(8,128)(2,1)S(1)}, bf16[416,256]{1,0:T(8,128)(2,1)}, u32[]{:S(2)}, u32[]{:S(2)}) collective-permute-start(bf16[416,256]{1,0:T(8,128)(2,1)S(1)} %shard_map.159.piece0), channel_id=1, source_target_pairs={{0,8},{4,12},{8,0},{12,4},{16,24},{20,28},{24,16},{28,20},{32,40},... | collective-permute-start | bytes 638984 | tf_op jit(solution)/shard_map/ppermute | solution.py:227
  113.3 10.3 %collective-permute-start.2 = (bf16[416,256]{1,0:T(8,128)(2,1)S(1)}, bf16[416,256]{1,0:T(8,128)(2,1)}, u32[]{:S(2)}, u32[]{:S(2)}) collective-permute-start(bf16[416,256]{1,0:T(8,128)(2,1)S(1)} %shard_map.159.piece0), channel_id=1, source_target_pairs={{0,12},{4,8},{8,4},{12,0},{16,28},{20,24},{24,20},{28,16},{32,44},... | collective-permute-start | bytes 638984 | tf_op jit(solution)/shard_map/ppermute | solution.py:227
  115.9 16.6 %all-to-all-start.5 = ((f32[4,24,512]{2,1,0:T(8,128)}), f32[4,24,512]{2,1,0:T(8,128)S(1)}, u32[]{:S(2)}, u32[]{:S(2)}) async-start(f32[4,24,512]{2,1,0:T(8,128)} %broadcast_in_dim.49), calls=%async_computation.5 | async-start | bytes 393216 | tf_op jit(solution)/shard_map/all_to_all | solution.py:220
  120.7 0.7 copy-start.9
  121.4 0.7 copy-start.11
  132.5 4.8 %copy-start.13 = (s32[4]{0:T(128)S(1)}, s32[4]{0:T(128)}, u32[]{:S(2)}) copy-start(s32[4]{0:T(128)} %param.28) | copy-start | bytes 52
  132.5 7.3 %copy-start.4 = (bf16[1,256,512]{2,1,0:T(8,128)(2,1)S(1)}, bf16[1,256,512]{2,1,0:T(8,128)(2,1)}, u32[]{:S(2)}) copy-start(bf16[1,256,512]{2,1,0:T(8,128)(2,1)} %param.22) | copy-start | bytes 786436
  132.5 14.0 %all-to-all-start.2 = ((bf16[4,272,256]{2,1,0:T(8,128)(2,1)}), bf16[4,272,256]{2,1,0:T(8,128)(2,1)S(1)}, u32[]{:S(2)}, u32[]{:S(2)}) async-start(bf16[4,272,256]{2,1,0:T(8,128)(2,1)} %shard_map.160), calls=%async_computation.2 | async-start | bytes 1114112 | tf_op jit(solution)/shard_map/all_to_all | solution.py:358
  139.8 0.7 copy-start.6

commit v2 on v1

--- a/solution.py
+++ b/solution.py
@@ -52,27 +52,61 @@
     )
 
 
+def prepare_kernel(owner_ref, slot_ref, state_ref, span_ref, pair_ref, crossing_ref, near_ref, tile_ref):
+    request = lax.axis_index("cache")
+
+    def held(index):
+        mine = owner_ref[index] == request
+        return jnp.where(mine, state_ref[slot_ref[index]], 0.0)
+
+    pair_ref[0] = held(request ^ 1)
+    pair_ref[1] = held(request ^ 3)
+    crossing_ref[...] = held(request ^ 2)
+    near_ref[...] = held(request)
+    tokens, heads = tile_ref.shape[0], span_ref.shape[0] // tile_ref.shape[0]
+    head = lax.axis_index("mp") >> 2
+    some = 32
+    rows = lax.broadcasted_iota(jnp.int32, (some, some * heads), 0)
+    columns = lax.broadcasted_iota(jnp.int32, (some, some * heads), 1)
+    pick = (columns == rows * heads + head).astype(jnp.float32).astype(jnp.bfloat16)
+    for at in range(tokens // some):
+        block = span_ref[at * some * heads : (at + 1) * some * heads, :]
+        tile_ref[at * some : (at + 1) * some, :] = jnp.dot(
+            pick, block, preferred_element_type=jnp.float32
+        ).astype(jnp.bfloat16)
+
+
 def attention_kernel(
-    info_ref, query_ref, piece0, piece1, piece2, piece3, span_ref, pos_ref, out_ref, kv_ref
+    prefix_ref, *refs
 ):
+    *queries, piece0, piece1, piece2, piece3, span_ref, out_ref, kv_ref = refs
     part_rows = piece0.shape[0]
     prefix_rows = 4 * part_rows
     tok_rows = span_ref.shape[0]
     for at, piece in enumerate((piece0, piece1, piece2, piece3)):
         kv_ref[at * part_rows : (at + 1) * part_rows, :] = piece[...]
     kv_ref[prefix_rows:, :] = span_ref[...]
-    seq_index, limit = info_ref[0], info_ref[1]
-    bias = jnp.where(pos_ref[...] < limit, 0.0, HIDDEN).astype(jnp.float32)
+    seq_index, limit = lax.axis_index("seq"), prefix_ref[lax.axis_index("cache")]
+    own_part = lax.axis_index("mp") & 3
+    pages = part_rows // 4
+    place = lax.broadcasted_iota(jnp.int32, (1, prefix_rows), 1)
+    piece = sum((place >= at * part_rows).astype(jnp.int32) for at in range(1, 4))
+    place = place - piece * part_rows
+    token = sum((place >= at * pages).astype(jnp.int32) for at in range(1, 4))
+    page = place - token * pages + seq_index * pages
+    position = page * 16 + (own_part ^ piece) * 4 + token
+    bias = jnp.where(position < limit, 0.0, HIDDEN).astype(jnp.float32)
     scale = LOG2E / math.sqrt(LANES)
     row = lax.broadcasted_iota(jnp.int32, (tok_rows, tok_rows), 0)
     column = lax.broadcasted_iota(jnp.int32, (tok_rows, tok_rows), 1)
     stat_row = lax.broadcasted_iota(jnp.int32, (STAT_ROWS, tok_rows), 0)
-    for group in range(query_ref.shape[0]):
+    for back, query_ref in enumerate(queries):
+        group = (seq_index - back) & 3
         seen = row - column + (group - seq_index) * tok_rows >= 0
         stats = jnp.zeros((STAT_ROWS, tok_rows), jnp.float32)
         for head in range(2):
             lanes = slice(head * LANES, (head + 1) * LANES)
-            query = query_ref[group, :, lanes]
+            query = query_ref[:, lanes]
             dims = (((1,), (1,)), ((), ()))
             far = lax.dot_general(
                 query, kv_ref[:prefix_rows, :LANES], dims, preferred_element_type=jnp.float32
@@ -185,15 +219,17 @@
 
 
 def full_scan_kernel(
-    info_ref, step_ref, input_ref, gate_ref, bc_ref, rate_ref, skip_ref, carry_ref, start_ref, out_ref
+    step_ref, input_ref, gate_ref, bc_ref, rate_ref, skip_ref, start_ref, *rest
 ):
+    *carries, out_ref = rest
     decay = rate_ref[...] * (-LOG2E)
     n_state = decay.shape[0]
     state = start_ref[...]
-    for group in range(carry_ref.shape[0] - 1):
-        factor = jnp.exp2(carry_ref[group, n_state : n_state + 1, :] * decay)
-        moved = factor * state + carry_ref[group, :n_state, :]
-        state = jnp.where(group < info_ref[0], moved, state)
+    for back in range(len(carries), 0, -1):
+        carry = carries[back - 1]
+        factor = jnp.exp2(carry[n_state : n_state + 1, :] * decay)
+        moved = factor * state + carry[:n_state, :]
+        state = jnp.where(back <= lax.axis_index("seq"), moved, state)
     skip = skip_ref[...]
 
     def read_out(start, inputs, values):
@@ -214,12 +250,13 @@
     )(*args)
 
 
-def shared_with(value, axis, groups=None):
-    count = len(groups[0]) if groups else lax.axis_size(axis)
-    everything = jnp.broadcast_to(value[None], (count,) + value.shape)
-    return lax.all_to_all(
-        everything, axis, split_axis=0, concat_axis=0, tiled=True, axis_index_groups=groups
-    )
+def shifted(value, axis, steps):
+    count = lax.axis_size(axis)
+    return lax.ppermute(value, axis, [(i, (i + steps) % count) for i in range(count)])
+
+
+def from_all(value, axis):
+    return [value] + [shifted(value, axis, steps) for steps in range(1, lax.axis_size(axis))]
 
 
 def swapped(value, flip):
@@ -252,7 +289,6 @@
     pages_dev = page_owner.shape[1] // n_seq
     sharers = n_mp // kv_heads
     page_part = page_len // sharers
-    head, part = mp_index // sharers, mp_index % sharers
 
     quarter_owner = lax.dynamic_slice_in_dim(page_owner[:, :, 0], seq_index * pages_dev, pages_dev, 1)
     quarter_slot = lax.dynamic_slice_in_dim(page_slot, seq_index * pages_dev, pages_dev, 1)
@@ -264,12 +300,26 @@
     hit = mine[:, None, :] & (rank[:, None, :] == places[None, :, None])
     chosen = jnp.sum(jnp.where(hit, quarter_slot[:, None, :], 0), axis=2).reshape(-1)
 
+    inputs = ssm_input[0]
+    sums = lax.dot_general(
+        bc_weight, inputs, (((0,), (1,)), ((), ())), preferred_element_type=jnp.float32
+    )
+    sums = jnp.broadcast_to(sums.astype(jnp.bfloat16)[None], (n_mp // 2,) + sums.shape)
+    sums, pool_kv = lax.optimization_barrier((sums, pool_kv))
+    chips = [[2 * chip + core for chip in range(n_mp // 2)] for core in range(2)]
+    sums = lax.all_to_all(
+        sums, "mp", split_axis=0, concat_axis=0, tiled=True, axis_index_groups=chips
+    )
     outgoing = call(
         pack_kernel,
         jax.ShapeDtypeStruct((n_cache, n_mp * 2 * page_part, width), jnp.bfloat16),
         [smem(), vmem()],
         (chosen, pool_kv.reshape(pool_pages, page_len * kv_heads, width)),
         24,
+    )
+
+    outgoing, sums, queries, state_pool = lax.optimization_barrier(
+        (outgoing, sums, queries, state_pool)
     )
     received = lax.all_to_all(
         outgoing.reshape(n_cache * n_mp, 2 * page_part, width),
@@ -278,22 +328,28 @@
         concat_axis=0,
         tiled=True,
     ).reshape(n_cache * n_mp * 2 * page_part, width)
-
-    all_queries = shared_with(queries[0], "seq")
-
-    inputs = ssm_input[0]
-    bc = lax.dot_general(
-        bc_weight, inputs, (((0,), (1,)), ((), ())), preferred_element_type=jnp.float32
-    )
-    near = [[base + i for i in range(8)] for base in range(0, n_mp, 8)]
-    across = [[base + i for i in range(0, n_mp, 8)] for base in range(8)]
-    bc = jnp.sum(shared_with(bc, "mp", near), axis=0)
-    bc = jnp.sum(shared_with(bc, "mp", across), axis=0)
-
-    states = state_pool.transpose(0, 2, 1)
-    leaving = jnp.where((state_owner == request)[:, None, None], states[state_slot], 0.0)
-    arriving = lax.all_to_all(leaving, "cache", split_axis=0, concat_axis=0, tiled=True)
-    start_state = lax.dynamic_index_in_dim(arriving, state_owner[request], 0, keepdims=False)
+    bc = jnp.sum(sums.astype(jnp.float32), axis=0)
+    bc = bc + swapped(bc, 1)
+
+    rate = decay_rate.T
+    state_shape = jax.ShapeDtypeStruct(rate.shape, jnp.float32)
+    pair, crossing, near_state, span_tile = pl.pallas_call(
+        prepare_kernel,
+        out_shape=(
+            jax.ShapeDtypeStruct((2,) + rate.shape, jnp.float32),
+            state_shape,
+            state_shape,
+            jax.ShapeDtypeStruct((tok_rows, width), jnp.bfloat16),
+        ),
+        in_specs=[smem(), smem(), vmem(), vmem()],
+        out_specs=(vmem(),) * 4,
+        compiler_params=params(24),
+    )(state_owner, state_slot, state_pool.transpose(0, 2, 1), span_kv.reshape(-1, width))
+    pair = lax.ppermute(pair, "cache", [(i, i ^ 1) for i in range(n_cache)])
+    crossing = crossing + pair[1]
+    near_state = near_state + pair[0]
+    all_queries = from_all(queries[0], "seq")
+    start_state = near_state + lax.ppermute(crossing, "cache", [(i, i ^ 2) for i in range(n_cache)])
 
     rate = decay_rate.T
     n_state = rate.shape[0]
@@ -304,56 +360,53 @@
         (time_step[0], inputs, bc, rate),
         24,
     )
-    carries = shared_with(carry, "seq")
+    last = shifted(carry, "seq", 1)
+    decay = jnp.exp2(carry[n_state : n_state + 1] * (rate * (-LOG2E)))
+    both = jnp.concatenate(
+        [decay * last[:n_state] + carry[:n_state], last[n_state:] + carry[n_state:]], axis=0
+    )
+    carries = [last, shifted(jnp.where(seq_index > 0, both, carry), "seq", 2)]
+    received, carries, start_state, bc, all_queries, span_tile = lax.optimization_barrier(
+        (received, carries, start_state, bc, all_queries, span_tile)
+    )
+    base = ((quarter_owner % n_cache) * n_mp + quarter_owner // n_cache) * 2 + rank
+    asked = jnp.arange(n_cache, dtype=jnp.int32)[:, None] == request
+    base = jnp.sum(jnp.where(asked, base, 0), axis=0) * page_part
+    tokens = jnp.arange(page_part, dtype=jnp.int32)
+    target = (base[None, :] + tokens[:, None]).reshape(-1, 1)
+    own = call(
+        compact_kernel,
+        jax.ShapeDtypeStruct((page_part * pages_dev, width), jnp.bfloat16),
+        [vmem()] * 2,
+        (target, received),
+        24,
+    )
+    across = swapped(own, 2)
+    pieces = [own, swapped(own, 1), across, swapped(across, 1)]
+    partial = call(
+        attention_kernel,
+        jax.ShapeDtypeStruct((n_seq, tok_rows + STAT_ROWS, queries.shape[2]), jnp.bfloat16),
+        [smem()] + [vmem()] * 9,
+        (prefix_len, *all_queries, *pieces, span_tile),
+        40,
+        [pltpu.VMEM((sharers * page_part * pages_dev + tok_rows, width), jnp.bfloat16)],
+    )
+    partial, bc, carries = lax.optimization_barrier((partial, bc, carries))
     ssm_out = call(
         full_scan_kernel,
         jax.ShapeDtypeStruct(inputs.shape, jnp.float32),
-        [smem()] + [vmem()] * 8,
+        [vmem()] * (7 + len(carries)),
         (
-            seq_index.reshape(1),
             time_step[0],
             inputs,
             gate_z[0],
             bc,
             rate,
             skip_gain.reshape(1, -1),
-            carries,
             start_state,
+            *carries,
         ),
         24,
-    )
-
-    my_owner = lax.dynamic_index_in_dim(quarter_owner, request, 0, keepdims=False)
-    my_rank = lax.dynamic_index_in_dim(rank, request, 0, keepdims=False)
-    base = ((my_owner % n_cache) * n_mp + my_owner // n_cache) * (2 * page_part) + my_rank * page_part
-    tokens = jnp.arange(page_part, dtype=jnp.int32)
-    target = (base[None, :] + tokens[:, None]).reshape(-1, 1)
-    page = seq_index * pages_dev + jnp.arange(pages_dev, dtype=jnp.int32)
-    in_page = (part ^ jnp.arange(sharers, dtype=jnp.int32))[:, None] * page_part + tokens[None, :]
-    position = (page[None, None, :] * page_len + in_page[:, :, None]).reshape(1, -1)
-
-    own = call(
-        compact_kernel,
-        jax.ShapeDtypeStruct((page_part * pages_dev, width), jnp.bfloat16),
-        [vmem()] * 2,
-        (target, received),
-        24,
-    )
-    pieces = [own] + [swapped(own, flip) for flip in range(1, sharers)]
-    span_tile = lax.dynamic_index_in_dim(span_kv[0], head, 1, keepdims=False)
-    partial = call(
-        attention_kernel,
-        jax.ShapeDtypeStruct((n_seq, tok_rows + STAT_ROWS, queries.shape[2]), jnp.bfloat16),
-        [smem()] + [vmem()] * 7,
-        (
-            jnp.stack([seq_index, prefix_len[request]]).astype(jnp.int32),
-            all_queries,
-            *pieces,
-            span_tile,
-            position,
-        ),
-        40,
-        [pltpu.VMEM((sharers * page_part * pages_dev + tok_rows, width), jnp.bfloat16)],
     )
     gathered = lax.all_to_all(partial, "seq", split_axis=0, concat_axis=0, tiled=True)
     attn_out = call(

time: 149 us -> 121 us (0.81)
  waiting for transfers between devices: 54.1 us -> 15.9 us
  starting transfers between devices: 54.8 us -> 74.8 us
  local copies, waits for them, and re-layouts: 9.58 us -> 4.74 us
  other arithmetic: 3.53 us -> 0.69 us
  between operations: 2.93 us -> 1.07 us
    all_to_all x1, waiting for transfers between devices: 32.1 us -> 0.01 us  [on_device(): lax.all_to_all(outgoing.reshape(n_cache * n_mp, 2 * page_part, width), ('...]
    ppermute x0 -> x7, starting transfers between devices: none -> 24.1 us  [the longest x5 16.5 us: shifted(): lax.ppermute(value, axis, [(i, (i + steps) % count) for i in range(count)])]
    all_to_all x5 -> x1, starting transfers between devices: 32.6 us -> 15.7 us  [on_device(): lax.all_to_all(sums, 'mp', split_axis=0, concat_axis=0, tiled=True, axis_...]
    all_to_all x5 -> x1, waiting for transfers between devices: 21.7 us -> 9.26 us  [on_device(): lax.all_to_all(sums, 'mp', split_axis=0, concat_axis=0, tiled=True, axis_...]
    all_to_all x1, starting transfers between devices: 8.37 us -> 15.7 us  [on_device(): lax.all_to_all(outgoing.reshape(n_cache * n_mp, 2 * page_part, width), ('...]
    ppermute x3 -> x4, starting transfers between devices: 9.02 us -> 15.7 us  [swapped(): lax.ppermute(value, 'mp', [(source, source ^ flip) for source in range(co...]
    all_to_all x1, waiting for transfers between devices: 0.09 us -> 2.98 us  [on_device(): lax.all_to_all(partial, 'seq', split_axis=0, concat_axis=0, tiled=True)]
    ppermute x0 -> x7, waiting for transfers between devices: none -> 2.82 us  [the longest x5 2.81 us: shifted(): lax.ppermute(value, axis, [(i, (i + steps) % count) for i in range(count)])]
  transfers between devices with their start and end apart: 10 -> 14, of which waited for: 6 -> 4; matrix products, arithmetic and copies ran while one was open for 6% -> 2% of each run, Pallas kernels for 14% -> 10%
where the time goes in v2:
time: 121 us; the launch traced here: 120 us
  starting transfers between devices  74.8 us (62%)
  Pallas kernels  21.9 us (18%)
  waiting for transfers between devices  15.9 us (13%)
  local copies, waits for them, and re-layouts  4.74 us (4%)
    pallas_call x6, Pallas kernels, call(): pl.pallas_call(kernel, out_shape=out, in_specs=specs, out_specs=vmem(), s...  21.1 us
    ppermute x5, starting transfers between devices, shifted(): lax.ppermute(value, axis, [(i, (i + steps) % count) for i in range(count)])  16.5 us
    all_to_all x1, starting transfers between devices, on_device(): lax.all_to_all(sums, 'mp', split_axis=0, concat_axis=0, tiled=True, axis_...  15.7 us
    ppermute x4, starting transfers between devices, swapped(): lax.ppermute(value, 'mp', [(source, source ^ flip) for source in range(co...  15.7 us
    all_to_all x1, starting transfers between devices, on_device(): lax.all_to_all(outgoing.reshape(n_cache * n_mp, 2 * page_part, width), ('...  15.7 us
    all_to_all x1, waiting for transfers between devices, on_device(): lax.all_to_all(sums, 'mp', split_axis=0, concat_axis=0, tiled=True, axis_...  9.26 us
    ppermute x1, starting transfers between devices, on_device(): lax.ppermute(crossing, 'cache', [(i, i ^ 2) for i in range(n_cache)])  4.74 us
    all_to_all x1, starting transfers between devices, on_device(): lax.all_to_all(partial, 'seq', split_axis=0, concat_axis=0, tiled=True)  3.6 us
  transfers between devices with their start and end apart: 14, of which 4 were waited for; matrix products, arithmetic and copies ran while one was open for 2% of the time, Pallas kernels for 10%

profile of v2, /device:TPU:1, one launch (start us, length us, event | category | flops | bytes accessed | tf_op | source)
XLA Modules:
  0.0 120.3 jit_solution(6928352197747971961)
XLA Ops:
  0.7 0.7 copy-done
  1.4 1.1 convolution_convert_fusion
  2.5 0.8 broadcast_in_dim.32
  3.3 15.7 %all-to-all-start = ((bf16[16,32,256]{2,1,0:T(8,128)(2,1)}), bf16[16,32,256]{2,1,0:T(8,128)(2,1)S(1)}, u32[]{:S(2)}, u32[]{:S(2)}) async-start(bf16[16,32,256]{2,1,0:T(8,128)(2,1)} %broadcast_in_dim.32), calls=%async_computation | async-start | bytes 524288 | tf_op jit(solution)/shard_map/all_to_all | solution.py:310
  19.0 0.8 constant_dynamic-slice_fusion.1
  19.8 0.8 constant_dynamic-slice_fusion
  21.2 1.7 %shard_map.158 = bf16[4,256,256]{2,1,0:T(8,128)(2,1)} custom-call(s32[8]{0:T(128)S(1)} %reshape.80.chosen_ref, bf16[16,128,256]{2,1,0:T(8,128)(2,1)S(1)} %bitcast.34), custom_call_target="tpu_custom_call" | custom-call | tf_op jit(solution)/shard_map/pallas_call | solution.py:243
  22.9 9.3 %all-to-all-done = bf16[16,32,256]{2,1,0:T(8,128)(2,1)S(1)} async-done(((bf16[16,32,256]{2,1,0:T(8,128)(2,1)}), bf16[16,32,256]{2,1,0:T(8,128)(2,1)S(1)}, u32[]{:S(2)}, u32[]{:S(2)}) %all-to-all-start) | async-done | bytes 262176 | tf_op jit(solution)/shard_map/all_to_all | solution.py:310
  32.2 15.7 %all-to-all-start.1 = ((bf16[128,8,256]{2,1,0:T(8,128)(2,1)}), bf16[128,8,256]{2,1,0:T(8,128)(2,1)S(1)}, u32[]{:S(2)}, u32[]{:S(2)}) async-start(bf16[128,8,256]{2,1,0:T(8,128)(2,1)} %bitcast.3), calls=%async_computation.1 | async-start | bytes 1048576 | tf_op jit(solution)/shard_map/all_to_all | solution.py:324
  48.0 2.9 %collective-permute-start = (f32[32,256]{1,0:T(8,128)S(1)}, f32[32,256]{1,0:T(8,128)S(1)}, u32[]{:S(2)}, u32[]{:S(2)}) collective-permute-start(f32[32,256]{1,0:T(8,128)S(1)} %convert_reduce_fusion), channel_id=1, source_target_pairs={{0,4},{4,0},{8,12},{12,8},{16,20},{20,16},{24,28},{28,24},{32,36},... | collective-permute-start | bytes 98312 | tf_op jit(solution)/shard_map/ppermute | solution.py:264
  51.1 4.6 %collective-permute-start.7 = (bf16[256,256]{1,0:T(8,128)(2,1)S(1)}, bf16[256,256]{1,0:T(8,128)(2,1)S(1)}, u32[]{:S(2)}, u32[]{:S(2)}) collective-permute-start(bf16[256,256]{1,0:T(8,128)(2,1)S(1)} %bitcast.39), channel_id=1, source_target_pairs={{0,384},{128,0},{256,128},{384,256},{1,385},{129,1},{257,129},{385... | collective-permute-start | bytes 393224 | tf_op jit(solution)/shard_map/ppermute | solution.py:255
  55.8 2.3 %collective-permute-start.6 = (bf16[256,256]{1,0:T(8,128)(2,1)S(1)}, bf16[256,256]{1,0:T(8,128)(2,1)S(1)}, u32[]{:S(2)}, u32[]{:S(2)}) collective-permute-start(bf16[256,256]{1,0:T(8,128)(2,1)S(1)} %bitcast.40), channel_id=1, source_target_pairs={{0,256},{128,384},{256,0},{384,128},{1,257},{129,385},{257,1},{385... | collective-permute-start | bytes 393224 | tf_op jit(solution)/shard_map/ppermute | solution.py:255
  58.1 2.6 %collective-permute-start.5 = (bf16[256,256]{1,0:T(8,128)(2,1)S(1)}, bf16[256,256]{1,0:T(8,128)(2,1)S(1)}, u32[]{:S(2)}, u32[]{:S(2)}) collective-permute-start(bf16[256,256]{1,0:T(8,128)(2,1)S(1)} %bitcast.41), channel_id=1, source_target_pairs={{0,128},{128,256},{256,384},{384,0},{1,129},{129,257},{257,385},{3... | collective-permute-start | bytes 393224 | tf_op jit(solution)/shard_map/ppermute | solution.py:255
  60.7 0.6 copy-done.10
  61.3 0.8 shard_map.160
  62.2 2.9 %collective-permute-start.3 = (f32[2,16,512]{2,1,0:T(8,128)S(1)}, f32[2,16,512]{2,1,0:T(8,128)S(1)}, u32[]{:S(2)}, u32[]{:S(2)}) collective-permute-start(f32[2,16,512]{2,1,0:T(8,128)S(1)} %get-tuple-element.32), channel_id=1, source_target_pairs={{0,1},{1,0},{2,3},{3,2},{4,5},{5,4},{6,7},{7,6},{8,9},{9,8},{10,11... | collective-permute-start | bytes 196616 | tf_op jit(solution)/shard_map/ppermute | solution.py:348
  65.1 3.3 %shard_map.159 = f32[24,512]{1,0:T(8,128)S(1)} custom-call(f32[256,512]{1,0:T(8,128)S(1)} %bitcast.31, bf16[256,512]{1,0:T(8,128)(2,1)S(1)} %bitcast.29, f32[32,256]{1,0:T(8,128)S(1)} %add.74.bc_ref, f32[16,512]{1,0:T(8,128)S(1)} %bitcast.36), custom_call_target="tpu_custom_call" | custom-call | tf_op jit(solution)/shard_map/pallas_call | solution.py:243
  68.5 3.5 %collective-permute-start.1 = (f32[24,512]{1,0:T(8,128)S(1)}, f32[24,512]{1,0:T(8,128)S(1)}, u32[]{:S(2)}, u32[]{:S(2)}) collective-permute-start(f32[24,512]{1,0:T(8,128)S(1)} %shard_map.159), channel_id=1, source_target_pairs={{0,128},{128,256},{256,384},{384,0},{1,129},{129,257},{257,385},{3... | collective-permute-start | bytes 147464 | tf_op jit(solution)/shard_map/ppermute | solution.py:255
  72.0 4.7 %collective-permute-start.4 = (f32[16,512]{1,0:T(8,128)S(1)}, f32[16,512]{1,0:T(8,128)S(1)}, u32[]{:S(2)}, u32[]{:S(2)}) collective-permute-start(f32[16,512]{1,0:T(8,128)S(1)} %fusion), channel_id=1, source_target_pairs={{0,2},{1,3},{2,0},{3,1},{4,6},{5,7},{6,4},{7,5},{8,10},{9,11},{10,... | collective-permute-start | bytes 98312 | tf_op jit(solution)/shard_map/ppermute | solution.py:352
  76.8 3.5 %collective-permute-start.2 = (f32[24,512]{1,0:T(8,128)S(1)}, f32[24,512]{1,0:T(8,128)S(1)}, u32[]{:S(2)}, u32[]{:S(2)}) collective-permute-start(f32[24,512]{1,0:T(8,128)S(1)} %maximum_select_fusion), channel_id=1, source_target_pairs={{0,256},{128,384},{256,0},{384,128},{1,257},{129,385},{257,1},{385... | collective-permute-start | bytes 147464 | tf_op jit(solution)/shard_map/ppermute | solution.py:255
  80.4 2.8 %collective-permute-done.2.rest_1_ = f32[24,512]{1,0:T(8,128)S(1)} collective-permute-done((f32[24,512]{1,0:T(8,128)S(1)}, f32[24,512]{1,0:T(8,128)S(1)}, u32[]{:S(2)}, u32[]{:S(2)}) %collective-permute-start.2) | collective-permute-done | bytes 49184 | tf_op jit(solution)/shard_map/ppermute | solution.py:255
  83.2 0.5 shard_map.161.refs_4_
  83.7 3.1 %collective-permute-start.9 = (bf16[416,256]{1,0:T(8,128)(2,1)S(1)}, bf16[416,256]{1,0:T(8,128)(2,1)S(1)}, u32[]{:S(2)}, u32[]{:S(2)}) collective-permute-start(bf16[416,256]{1,0:T(8,128)(2,1)S(1)} %shard_map.161.refs_4_), channel_id=1, source_target_pairs={{0,8},{4,12},{8,0},{12,4},{16,24},{20,28},{24,16},{28,20},{32,40},... | collective-permute-start | bytes 638984 | tf_op jit(solution)/shard_map/ppermute | solution.py:264
  86.8 5.2 %collective-permute-start.8 = (bf16[416,256]{1,0:T(8,128)(2,1)S(1)}, bf16[416,256]{1,0:T(8,128)(2,1)S(1)}, u32[]{:S(2)}, u32[]{:S(2)}) collective-permute-start(bf16[416,256]{1,0:T(8,128)(2,1)S(1)} %shard_map.161.refs_4_), channel_id=1, source_target_pairs={{0,4},{4,0},{8,12},{12,8},{16,20},{20,16},{24,28},{28,24},{32,36},... | collective-permute-start | bytes 638984 | tf_op jit(solution)/shard_map/ppermute | solution.py:264
  92.0 4.5 %collective-permute-start.10 = (bf16[416,256]{1,0:T(8,128)(2,1)S(1)}, bf16[416,256]{1,0:T(8,128)(2,1)S(1)}, u32[]{:S(2)}, u32[]{:S(2)}) collective-permute-start(bf16[416,256]{1,0:T(8,128)(2,1)S(1)} %collective-permute-done.9.refs_6_), channel_id=1, source_target_pairs={{0,4},{4,0},{8,12},{12,8},{16,20},{20,16},{24,28},{28,24},{32,36},... | collective-permute-start | bytes 638984 | tf_op jit(solution)/shard_map/ppermute | solution.py:264
  96.5 0.9 collective-permute-done.10.refs_7_
  97.4 8.4 %shard_map.162 = bf16[4,272,256]{2,1,0:T(8,128)(2,1)} custom-call(s32[4]{0:T(128)S(1)} %copy-done.12, bf16[256,256]{1,0:T(8,128)(2,1)S(1)} %bitcast.42, bf16[256,256]{1,0:T(8,128)(2,1)S(1)} %collective-permute-done.5.refs_1_, bf16[256,256]{1,0:T(8,128)(2,1)S(1)} %collective-permute-done.6.refs_2_, bf16[256,256]{1,0:T(8,128)(2,1)S(1)} %collective-permute-done.7.refs_3_, ...), custom_call_target="tpu_custom_call" | custom-call | tf_op jit(solution)/shard_map/pallas_call | solution.py:243
  105.9 3.6 %all-to-all-start.2 = ((bf16[4,272,256]{2,1,0:T(8,128)(2,1)}), bf16[4,272,256]{2,1,0:T(8,128)(2,1)S(1)}, u32[]{:S(2)}, u32[]{:S(2)}) async-start(bf16[4,272,256]{2,1,0:T(8,128)(2,1)} %shard_map.162), calls=%async_computation.2 | async-start | bytes 1114112 | tf_op jit(solution)/shard_map/all_to_all | solution.py:411
  109.5 0.7 copy-done.9
  110.2 5.9 %shard_map.164 = f32[256,512]{1,0:T(8,128)} custom-call(f32[256,512]{1,0:T(8,128)S(1)} %bitcast.32, bf16[256,512]{1,0:T(8,128)(2,1)S(1)} %bitcast.30, bf16[256,512]{1,0:T(8,128)(2,1)S(1)} %bitcast.38, f32[32,256]{1,0:T(8,128)S(1)} %add.74.bc_ref, f32[16,512]{1,0:T(8,128)S(1)} %bitcast.37, f32[1,512]{1,0:T(1,128)S(1)} %bitcast.44, ...), custom_call_target="tpu_custom_call" | custom-call | tf_op jit(solution)/shard_map/pallas_call | solution.py:243
  116.1 3.0 %all-to-all-done.2.part_ref = bf16[4,272,256]{2,1,0:T(8,128)(2,1)S(1)} async-done(((bf16[4,272,256]{2,1,0:T(8,128)(2,1)}), bf16[4,272,256]{2,1,0:T(8,128)(2,1)S(1)}, u32[]{:S(2)}, u32[]{:S(2)}) %all-to-all-start.2) | async-done | bytes 557088 | tf_op jit(solution)/shard_map/all_to_all | solution.py:411
  119.0 1.3 %shard_map.163 = f32[256,256]{1,0:T(8,128)} custom-call(bf16[4,272,256]{2,1,0:T(8,128)(2,1)S(1)} %all-to-all-done.2.part_ref), custom_call_target="tpu_custom_call" | custom-call | tf_op jit(solution)/shard_map/pallas_call | solution.py:243
  (53 shorter events, 1.1 us)
Async XLA Ops:
  0.6 0.8 copy-start
  0.6 20.6 %copy-start.3 = (bf16[16,16,8,256]{3,2,1,0:T(8,128)(2,1)S(1)}, bf16[16,16,8,256]{3,2,1,0:T(8,128)(2,1)}, u32[]{:S(2)}) copy-start(bf16[16,16,8,256]{3,2,1,0:T(8,128)(2,1)} %param.17) | copy-start | bytes 3145732
  3.3 28.9 %all-to-all-start = ((bf16[16,32,256]{2,1,0:T(8,128)(2,1)}), bf16[16,32,256]{2,1,0:T(8,128)(2,1)S(1)}, u32[]{:S(2)}, u32[]{:S(2)}) async-start(bf16[16,32,256]{2,1,0:T(8,128)(2,1)} %broadcast_in_dim.32), calls=%async_computation | async-start | bytes 524288 | tf_op jit(solution)/shard_map/all_to_all | solution.py:310
  22.9 37.8 %copy-start.4 = (bf16[1,256,8,256]{3,2,1,0:T(8,128)(2,1)S(1)}, bf16[1,256,8,256]{3,2,1,0:T(8,128)(2,1)}, u32[]{:S(2)}) copy-start(bf16[1,256,8,256]{3,2,1,0:T(8,128)(2,1)} %param.16) | copy-start | bytes 3145732
  32.2 51.0 %all-to-all-start.1 = ((bf16[128,8,256]{2,1,0:T(8,128)(2,1)}), bf16[128,8,256]{2,1,0:T(8,128)(2,1)S(1)}, u32[]{:S(2)}, u32[]{:S(2)}) async-start(bf16[128,8,256]{2,1,0:T(8,128)(2,1)} %bitcast.3), calls=%async_computation.1 | async-start | bytes 1048576 | tf_op jit(solution)/shard_map/all_to_all | solution.py:324
  47.9 12.8 %copy-start.8 = (f32[4,512,16]{1,2,0:T(8,128)S(1)}, f32[4,512,16]{1,2,0:T(8,128)}, u32[]{:S(2)}) copy-start(f32[4,512,16]{1,2,0:T(8,128)} %param.27) | copy-start | bytes 393220
  48.0 3.2 %copy-start.7 = (bf16[1,256,256]{2,1,0:T(8,128)(2,1)S(1)}, bf16[1,256,256]{2,1,0:T(8,128)(2,1)}, u32[]{:S(2)}) copy-start(bf16[1,256,256]{2,1,0:T(8,128)(2,1)} %param.15) | copy-start | bytes 393220
  48.0 17.1 %collective-permute-start = (f32[32,256]{1,0:T(8,128)S(1)}, f32[32,256]{1,0:T(8,128)S(1)}, u32[]{:S(2)}, u32[]{:S(2)}) collective-permute-start(f32[32,256]{1,0:T(8,128)S(1)} %convert_reduce_fusion), channel_id=1, source_target_pairs={{0,4},{4,0},{8,12},{12,8},{16,20},{20,16},{24,28},{28,24},{32,36},... | collective-permute-start | bytes 98312 | tf_op jit(solution)/shard_map/ppermute | solution.py:264
  51.1 29.2 %collective-permute-start.7 = (bf16[256,256]{1,0:T(8,128)(2,1)S(1)}, bf16[256,256]{1,0:T(8,128)(2,1)S(1)}, u32[]{:S(2)}, u32[]{:S(2)}) collective-permute-start(bf16[256,256]{1,0:T(8,128)(2,1)S(1)} %bitcast.39), channel_id=1, source_target_pairs={{0,384},{128,0},{256,128},{384,256},{1,385},{129,1},{257,129},{385... | collective-permute-start | bytes 393224 | tf_op jit(solution)/shard_map/ppermute | solution.py:255
  55.8 24.6 %collective-permute-start.6 = (bf16[256,256]{1,0:T(8,128)(2,1)S(1)}, bf16[256,256]{1,0:T(8,128)(2,1)S(1)}, u32[]{:S(2)}, u32[]{:S(2)}) collective-permute-start(bf16[256,256]{1,0:T(8,128)(2,1)S(1)} %bitcast.40), channel_id=1, source_target_pairs={{0,256},{128,384},{256,0},{384,128},{1,257},{129,385},{257,1},{385... | collective-permute-start | bytes 393224 | tf_op jit(solution)/shard_map/ppermute | solution.py:255
  58.1 22.3 %collective-permute-start.5 = (bf16[256,256]{1,0:T(8,128)(2,1)S(1)}, bf16[256,256]{1,0:T(8,128)(2,1)S(1)}, u32[]{:S(2)}, u32[]{:S(2)}) collective-permute-start(bf16[256,256]{1,0:T(8,128)(2,1)S(1)} %bitcast.41), channel_id=1, source_target_pairs={{0,128},{128,256},{256,384},{384,0},{1,129},{129,257},{257,385},{3... | collective-permute-start | bytes 393224 | tf_op jit(solution)/shard_map/ppermute | solution.py:255
  60.7 0.7 copy-start.10
  60.7 0.7 copy-start.11
  61.3 3.7 %copy-start.1 = (bf16[1,256,512]{2,1,0:T(8,128)(2,1)S(1)}, bf16[1,256,512]{2,1,0:T(8,128)(2,1)}, u32[]{:S(2)}) copy-start(bf16[1,256,512]{2,1,0:T(8,128)(2,1)} %param.21) | copy-start | bytes 786436
  61.3 3.7 %copy-start.2 = (f32[1,256,512]{2,1,0:T(8,128)S(1)}, f32[1,256,512]{2,1,0:T(8,128)}, u32[]{:S(2)}) copy-start(f32[1,256,512]{2,1,0:T(8,128)} %param.23) | copy-start | bytes 1572868
  62.2 2.9 %copy-start.5 = (f32[512,16]{0,1:T(8,128)S(1)}, f32[512,16]{0,1:T(8,128)}, u32[]{:S(2)}) copy-start(f32[512,16]{0,1:T(8,128)} %param.25) | copy-start | bytes 98308
  62.2 9.8 %collective-permute-start.3 = (f32[2,16,512]{2,1,0:T(8,128)S(1)}, f32[2,16,512]{2,1,0:T(8,128)S(1)}, u32[]{:S(2)}, u32[]{:S(2)}) collective-permute-start(f32[2,16,512]{2,1,0:T(8,128)S(1)} %get-tuple-element.32), channel_id=1, source_target_pairs={{0,1},{1,0},{2,3},{3,2},{4,5},{5,4},{6,7},{7,6},{8,9},{9,8},{10,11... | collective-permute-start | bytes 196616 | tf_op jit(solution)/shard_map/ppermute | solution.py:348
  68.5 8.3 %collective-permute-start.1 = (f32[24,512]{1,0:T(8,128)S(1)}, f32[24,512]{1,0:T(8,128)S(1)}, u32[]{:S(2)}, u32[]{:S(2)}) collective-permute-start(f32[24,512]{1,0:T(8,128)S(1)} %shard_map.159), channel_id=1, source_target_pairs={{0,128},{128,256},{256,384},{384,0},{1,129},{129,257},{257,385},{3... | collective-permute-start | bytes 147464 | tf_op jit(solution)/shard_map/ppermute | solution.py:255
  72.0 8.3 %collective-permute-start.4 = (f32[16,512]{1,0:T(8,128)S(1)}, f32[16,512]{1,0:T(8,128)S(1)}, u32[]{:S(2)}, u32[]{:S(2)}) collective-permute-start(f32[16,512]{1,0:T(8,128)S(1)} %fusion), channel_id=1, source_target_pairs={{0,2},{1,3},{2,0},{3,1},{4,6},{5,7},{6,4},{7,5},{8,10},{9,11},{10,... | collective-permute-start | bytes 98312 | tf_op jit(solution)/shard_map/ppermute | solution.py:352
  76.8 6.3 %collective-permute-start.2 = (f32[24,512]{1,0:T(8,128)S(1)}, f32[24,512]{1,0:T(8,128)S(1)}, u32[]{:S(2)}, u32[]{:S(2)}) collective-permute-start(f32[24,512]{1,0:T(8,128)S(1)} %maximum_select_fusion), channel_id=1, source_target_pairs={{0,256},{128,384},{256,0},{384,128},{1,257},{129,385},{257,1},{385... | collective-permute-start | bytes 147464 | tf_op jit(solution)/shard_map/ppermute | solution.py:255
  83.2 14.2 %copy-start.12 = (s32[4]{0:T(128)S(1)}, s32[4]{0:T(128)}, u32[]{:S(2)}) copy-start(s32[4]{0:T(128)} %prefix_ref.1) | copy-start | bytes 52
  83.7 8.3 %collective-permute-start.9 = (bf16[416,256]{1,0:T(8,128)(2,1)S(1)}, bf16[416,256]{1,0:T(8,128)(2,1)S(1)}, u32[]{:S(2)}, u32[]{:S(2)}) collective-permute-start(bf16[416,256]{1,0:T(8,128)(2,1)S(1)} %shard_map.161.refs_4_), channel_id=1, source_target_pairs={{0,8},{4,12},{8,0},{12,4},{16,24},{20,28},{24,16},{28,20},{32,40},... | collective-permute-start | bytes 638984 | tf_op jit(solution)/shard_map/ppermute | solution.py:264
  86.8 9.7 %collective-permute-start.8 = (bf16[416,256]{1,0:T(8,128)(2,1)S(1)}, bf16[416,256]{1,0:T(8,128)(2,1)S(1)}, u32[]{:S(2)}, u32[]{:S(2)}) collective-permute-start(bf16[416,256]{1,0:T(8,128)(2,1)S(1)} %shard_map.161.refs_4_), channel_id=1, source_target_pairs={{0,4},{4,0},{8,12},{12,8},{16,20},{20,16},{24,28},{28,24},{32,36},... | collective-permute-start | bytes 638984 | tf_op jit(solution)/shard_map/ppermute | solution.py:264
  92.0 5.4 %collective-permute-start.10 = (bf16[416,256]{1,0:T(8,128)(2,1)S(1)}, bf16[416,256]{1,0:T(8,128)(2,1)S(1)}, u32[]{:S(2)}, u32[]{:S(2)}) collective-permute-start(bf16[416,256]{1,0:T(8,128)(2,1)S(1)} %collective-permute-done.9.refs_6_), channel_id=1, source_target_pairs={{0,4},{4,0},{8,12},{12,8},{16,20},{20,16},{24,28},{28,24},{32,36},... | collective-permute-start | bytes 638984 | tf_op jit(solution)/shard_map/ppermute | solution.py:264
  105.9 3.6 %copy-start.6 = (bf16[1,256,512]{2,1,0:T(8,128)(2,1)S(1)}, bf16[1,256,512]{2,1,0:T(8,128)(2,1)}, u32[]{:S(2)}) copy-start(bf16[1,256,512]{2,1,0:T(8,128)(2,1)} %param.22) | copy-start | bytes 786436
  105.9 13.2 %all-to-all-start.2 = ((bf16[4,272,256]{2,1,0:T(8,128)(2,1)}), bf16[4,272,256]{2,1,0:T(8,128)(2,1)S(1)}, u32[]{:S(2)}, u32[]{:S(2)}) async-start(bf16[4,272,256]{2,1,0:T(8,128)(2,1)} %shard_map.162), calls=%async_computation.2 | async-start | bytes 1114112 | tf_op jit(solution)/shard_map/all_to_all | solution.py:411
  109.5 0.7 copy-start.9

commit v3 on v2

--- a/solution.py
+++ b/solution.py
@@ -97,48 +97,49 @@
     position = page * 16 + (own_part ^ piece) * 4 + token
     bias = jnp.where(position < limit, 0.0, HIDDEN).astype(jnp.float32)
     scale = LOG2E / math.sqrt(LANES)
-    row = lax.broadcasted_iota(jnp.int32, (tok_rows, tok_rows), 0)
-    column = lax.broadcasted_iota(jnp.int32, (tok_rows, tok_rows), 1)
+    row = lax.broadcasted_iota(jnp.int32, (2 * tok_rows, tok_rows), 0) & (tok_rows - 1)
+    column = lax.broadcasted_iota(jnp.int32, (2 * tok_rows, tok_rows), 1)
     stat_row = lax.broadcasted_iota(jnp.int32, (STAT_ROWS, tok_rows), 0)
+    dims = (((1,), (1,)), ((), ()))
     for back, query_ref in enumerate(queries):
         group = (seq_index - back) & 3
         seen = row - column + (group - seq_index) * tok_rows >= 0
+        query = jnp.concatenate([query_ref[:, :LANES], query_ref[:, LANES:]], axis=0)
+        far = lax.dot_general(
+            query, kv_ref[:prefix_rows, :LANES], dims, preferred_element_type=jnp.float32
+        )
+        near = lax.dot_general(
+            query, kv_ref[prefix_rows:, :LANES], dims, preferred_element_type=jnp.float32
+        )
+        far = far * scale + bias
+        near = jnp.where(seen, near * scale, HIDDEN)
+        top = jnp.maximum(
+            jnp.max(far, axis=1, keepdims=True), jnp.max(near, axis=1, keepdims=True)
+        )
+        top = jnp.maximum(top, FLOOR)
+        far = jnp.exp2(far - top)
+        near = jnp.exp2(near - top)
+        total = jnp.sum(far, axis=1, keepdims=True) + jnp.sum(near, axis=1, keepdims=True)
+        total = jnp.maximum(total, 1e-37)
+        mixed = jnp.dot(
+            far.astype(jnp.bfloat16),
+            kv_ref[:prefix_rows, LANES:],
+            preferred_element_type=jnp.float32,
+        ) + jnp.dot(
+            near.astype(jnp.bfloat16),
+            kv_ref[prefix_rows:, LANES:],
+            preferred_element_type=jnp.float32,
+        )
+        mixed = (mixed / total).astype(jnp.bfloat16)
+        level = top + jnp.log2(total)
         stats = jnp.zeros((STAT_ROWS, tok_rows), jnp.float32)
         for head in range(2):
-            lanes = slice(head * LANES, (head + 1) * LANES)
-            query = query_ref[:, lanes]
-            dims = (((1,), (1,)), ((), ()))
-            far = lax.dot_general(
-                query, kv_ref[:prefix_rows, :LANES], dims, preferred_element_type=jnp.float32
-            )
-            near = lax.dot_general(
-                query, kv_ref[prefix_rows:, :LANES], dims, preferred_element_type=jnp.float32
-            )
-            far = far * scale + bias
-            near = jnp.where(seen, near * scale, HIDDEN)
-            top = jnp.maximum(
-                jnp.max(far, axis=1, keepdims=True), jnp.max(near, axis=1, keepdims=True)
-            )
-            top = jnp.maximum(top, FLOOR)
-            far = jnp.exp2(far - top)
-            near = jnp.exp2(near - top)
-            total = jnp.sum(far, axis=1, keepdims=True) + jnp.sum(near, axis=1, keepdims=True)
-            total = jnp.maximum(total, 1e-37)
-            mixed = jnp.dot(
-                far.astype(jnp.bfloat16),
-                kv_ref[:prefix_rows, LANES:],
-                preferred_element_type=jnp.float32,
-            ) + jnp.dot(
-                near.astype(jnp.bfloat16),
-                kv_ref[prefix_rows:, LANES:],
-                preferred_element_type=jnp.float32,
-            )
-            out_ref[group, :tok_rows, lanes] = (mixed / total).astype(jnp.bfloat16)
-            level = top + jnp.log2(total)
-            level = jnp.transpose(jnp.broadcast_to(level, (tok_rows, LANES)))[:STAT_ROWS]
-            high = level.astype(jnp.bfloat16).astype(jnp.float32)
-            middle = (level - high).astype(jnp.bfloat16).astype(jnp.float32)
-            low = level - high - middle
+            rows = slice(head * tok_rows, (head + 1) * tok_rows)
+            out_ref[group, :tok_rows, head * LANES : (head + 1) * LANES] = mixed[rows]
+            turned = jnp.transpose(jnp.broadcast_to(level[rows], (tok_rows, LANES)))[:STAT_ROWS]
+            high = turned.astype(jnp.bfloat16).astype(jnp.float32)
+            middle = (turned - high).astype(jnp.bfloat16).astype(jnp.float32)
+            low = turned - high - middle
             for at, value in enumerate((high, middle, low)):
                 stats = jnp.where(stat_row == 3 * head + at, value, stats)
         out_ref[group, tok_rows:, :] = stats.astype(jnp.bfloat16)

time: 121 us -> 121 us (level)
  no operation moved by 1% of the time
where the time goes in v3:
time: 121 us; the launch traced here: 120 us
  starting transfers between devices  74.8 us (62%)
  Pallas kernels  21.7 us (18%)
  waiting for transfers between devices  15.9 us (13%)
  local copies, waits for them, and re-layouts  4.74 us (4%)
    pallas_call x6, Pallas kernels, call(): pl.pallas_call(kernel, out_shape=out, in_specs=specs, out_specs=vmem(), s...  20.9 us
    ppermute x5, starting transfers between devices, shifted(): lax.ppermute(value, axis, [(i, (i + steps) % count) for i in range(count)])  16.5 us
    all_to_all x1, starting transfers between devices, on_device(): lax.all_to_all(sums, 'mp', split_axis=0, concat_axis=0, tiled=True, axis_...  15.7 us
    ppermute x4, starting transfers between devices, swapped(): lax.ppermute(value, 'mp', [(source, source ^ flip) for source in range(co...  15.7 us
    all_to_all x1, starting transfers between devices, on_device(): lax.all_to_all(outgoing.reshape(n_cache * n_mp, 2 * page_part, width), ('...  15.7 us
    all_to_all x1, waiting for transfers between devices, on_device(): lax.all_to_all(sums, 'mp', split_axis=0, concat_axis=0, tiled=True, axis_...  9.26 us
    ppermute x1, starting transfers between devices, on_device(): lax.ppermute(crossing, 'cache', [(i, i ^ 2) for i in range(n_cache)])  4.74 us
    all_to_all x1, starting transfers between devices, on_device(): lax.all_to_all(partial, 'seq', split_axis=0, concat_axis=0, tiled=True)  3.6 us
  transfers between devices with their start and end apart: 14, of which 4 were waited for; matrix products, arithmetic and copies ran while one was open for 2% of the time, Pallas kernels for 10%

profile of v3, /device:TPU:1, one launch (start us, length us, event | category | flops | bytes accessed | tf_op | source)
XLA Modules:
  0.0 120.1 jit_solution(5239887016012395713)
XLA Ops:
  0.7 0.7 copy-done
  1.4 1.1 convolution_convert_fusion
  2.5 0.8 broadcast_in_dim.32
  3.3 15.7 %all-to-all-start = ((bf16[16,32,256]{2,1,0:T(8,128)(2,1)}), bf16[16,32,256]{2,1,0:T(8,128)(2,1)S(1)}, u32[]{:S(2)}, u32[]{:S(2)}) async-start(bf16[16,32,256]{2,1,0:T(8,128)(2,1)} %broadcast_in_dim.32), calls=%async_computation | async-start | bytes 524288 | tf_op jit(solution)/shard_map/all_to_all | solution.py:311
  19.0 0.8 constant_dynamic-slice_fusion.1
  19.8 0.8 constant_dynamic-slice_fusion
  21.2 1.7 %shard_map.158 = bf16[4,256,256]{2,1,0:T(8,128)(2,1)} custom-call(s32[8]{0:T(128)S(1)} %reshape.80.chosen_ref, bf16[16,128,256]{2,1,0:T(8,128)(2,1)S(1)} %bitcast.34), custom_call_target="tpu_custom_call" | custom-call | tf_op jit(solution)/shard_map/pallas_call | solution.py:244
  22.9 9.3 %all-to-all-done = bf16[16,32,256]{2,1,0:T(8,128)(2,1)S(1)} async-done(((bf16[16,32,256]{2,1,0:T(8,128)(2,1)}), bf16[16,32,256]{2,1,0:T(8,128)(2,1)S(1)}, u32[]{:S(2)}, u32[]{:S(2)}) %all-to-all-start) | async-done | bytes 262176 | tf_op jit(solution)/shard_map/all_to_all | solution.py:311
  32.2 15.7 %all-to-all-start.1 = ((bf16[128,8,256]{2,1,0:T(8,128)(2,1)}), bf16[128,8,256]{2,1,0:T(8,128)(2,1)S(1)}, u32[]{:S(2)}, u32[]{:S(2)}) async-start(bf16[128,8,256]{2,1,0:T(8,128)(2,1)} %bitcast.3), calls=%async_computation.1 | async-start | bytes 1048576 | tf_op jit(solution)/shard_map/all_to_all | solution.py:325
  48.0 2.9 %collective-permute-start = (f32[32,256]{1,0:T(8,128)S(1)}, f32[32,256]{1,0:T(8,128)S(1)}, u32[]{:S(2)}, u32[]{:S(2)}) collective-permute-start(f32[32,256]{1,0:T(8,128)S(1)} %convert_reduce_fusion), channel_id=1, source_target_pairs={{0,4},{4,0},{8,12},{12,8},{16,20},{20,16},{24,28},{28,24},{32,36},... | collective-permute-start | bytes 98312 | tf_op jit(solution)/shard_map/ppermute | solution.py:265
  51.1 4.6 %collective-permute-start.7 = (bf16[256,256]{1,0:T(8,128)(2,1)S(1)}, bf16[256,256]{1,0:T(8,128)(2,1)S(1)}, u32[]{:S(2)}, u32[]{:S(2)}) collective-permute-start(bf16[256,256]{1,0:T(8,128)(2,1)S(1)} %bitcast.39), channel_id=1, source_target_pairs={{0,384},{128,0},{256,128},{384,256},{1,385},{129,1},{257,129},{385... | collective-permute-start | bytes 393224 | tf_op jit(solution)/shard_map/ppermute | solution.py:256
  55.8 2.3 %collective-permute-start.6 = (bf16[256,256]{1,0:T(8,128)(2,1)S(1)}, bf16[256,256]{1,0:T(8,128)(2,1)S(1)}, u32[]{:S(2)}, u32[]{:S(2)}) collective-permute-start(bf16[256,256]{1,0:T(8,128)(2,1)S(1)} %bitcast.40), channel_id=1, source_target_pairs={{0,256},{128,384},{256,0},{384,128},{1,257},{129,385},{257,1},{385... | collective-permute-start | bytes 393224 | tf_op jit(solution)/shard_map/ppermute | solution.py:256
  58.1 2.6 %collective-permute-start.5 = (bf16[256,256]{1,0:T(8,128)(2,1)S(1)}, bf16[256,256]{1,0:T(8,128)(2,1)S(1)}, u32[]{:S(2)}, u32[]{:S(2)}) collective-permute-start(bf16[256,256]{1,0:T(8,128)(2,1)S(1)} %bitcast.41), channel_id=1, source_target_pairs={{0,128},{128,256},{256,384},{384,0},{1,129},{129,257},{257,385},{3... | collective-permute-start | bytes 393224 | tf_op jit(solution)/shard_map/ppermute | solution.py:256
  60.7 0.6 copy-done.10
  61.3 0.8 shard_map.160
  62.2 2.9 %collective-permute-start.3 = (f32[2,16,512]{2,1,0:T(8,128)S(1)}, f32[2,16,512]{2,1,0:T(8,128)S(1)}, u32[]{:S(2)}, u32[]{:S(2)}) collective-permute-start(f32[2,16,512]{2,1,0:T(8,128)S(1)} %get-tuple-element.32), channel_id=1, source_target_pairs={{0,1},{1,0},{2,3},{3,2},{4,5},{5,4},{6,7},{7,6},{8,9},{9,8},{10,11... | collective-permute-start | bytes 196616 | tf_op jit(solution)/shard_map/ppermute | solution.py:349
  65.1 3.3 %shard_map.159 = f32[24,512]{1,0:T(8,128)S(1)} custom-call(f32[256,512]{1,0:T(8,128)S(1)} %bitcast.31, bf16[256,512]{1,0:T(8,128)(2,1)S(1)} %bitcast.29, f32[32,256]{1,0:T(8,128)S(1)} %add.74.bc_ref, f32[16,512]{1,0:T(8,128)S(1)} %bitcast.36), custom_call_target="tpu_custom_call" | custom-call | tf_op jit(solution)/shard_map/pallas_call | solution.py:244
  68.5 3.5 %collective-permute-start.1 = (f32[24,512]{1,0:T(8,128)S(1)}, f32[24,512]{1,0:T(8,128)S(1)}, u32[]{:S(2)}, u32[]{:S(2)}) collective-permute-start(f32[24,512]{1,0:T(8,128)S(1)} %shard_map.159), channel_id=1, source_target_pairs={{0,128},{128,256},{256,384},{384,0},{1,129},{129,257},{257,385},{3... | collective-permute-start | bytes 147464 | tf_op jit(solution)/shard_map/ppermute | solution.py:256
  72.0 4.7 %collective-permute-start.4 = (f32[16,512]{1,0:T(8,128)S(1)}, f32[16,512]{1,0:T(8,128)S(1)}, u32[]{:S(2)}, u32[]{:S(2)}) collective-permute-start(f32[16,512]{1,0:T(8,128)S(1)} %fusion), channel_id=1, source_target_pairs={{0,2},{1,3},{2,0},{3,1},{4,6},{5,7},{6,4},{7,5},{8,10},{9,11},{10,... | collective-permute-start | bytes 98312 | tf_op jit(solution)/shard_map/ppermute | solution.py:353
  76.8 3.5 %collective-permute-start.2 = (f32[24,512]{1,0:T(8,128)S(1)}, f32[24,512]{1,0:T(8,128)S(1)}, u32[]{:S(2)}, u32[]{:S(2)}) collective-permute-start(f32[24,512]{1,0:T(8,128)S(1)} %maximum_select_fusion), channel_id=1, source_target_pairs={{0,256},{128,384},{256,0},{384,128},{1,257},{129,385},{257,1},{385... | collective-permute-start | bytes 147464 | tf_op jit(solution)/shard_map/ppermute | solution.py:256
  80.4 2.8 %collective-permute-done.2.rest_1_ = f32[24,512]{1,0:T(8,128)S(1)} collective-permute-done((f32[24,512]{1,0:T(8,128)S(1)}, f32[24,512]{1,0:T(8,128)S(1)}, u32[]{:S(2)}, u32[]{:S(2)}) %collective-permute-start.2) | collective-permute-done | bytes 49184 | tf_op jit(solution)/shard_map/ppermute | solution.py:256
  83.2 0.5 shard_map.161.refs_4_
  83.7 3.1 %collective-permute-start.9 = (bf16[416,256]{1,0:T(8,128)(2,1)S(1)}, bf16[416,256]{1,0:T(8,128)(2,1)S(1)}, u32[]{:S(2)}, u32[]{:S(2)}) collective-permute-start(bf16[416,256]{1,0:T(8,128)(2,1)S(1)} %shard_map.161.refs_4_), channel_id=1, source_target_pairs={{0,8},{4,12},{8,0},{12,4},{16,24},{20,28},{24,16},{28,20},{32,40},... | collective-permute-start | bytes 638984 | tf_op jit(solution)/shard_map/ppermute | solution.py:265
  86.8 5.2 %collective-permute-start.8 = (bf16[416,256]{1,0:T(8,128)(2,1)S(1)}, bf16[416,256]{1,0:T(8,128)(2,1)S(1)}, u32[]{:S(2)}, u32[]{:S(2)}) collective-permute-start(bf16[416,256]{1,0:T(8,128)(2,1)S(1)} %shard_map.161.refs_4_), channel_id=1, source_target_pairs={{0,4},{4,0},{8,12},{12,8},{16,20},{20,16},{24,28},{28,24},{32,36},... | collective-permute-start | bytes 638984 | tf_op jit(solution)/shard_map/ppermute | solution.py:265
  92.0 4.5 %collective-permute-start.10 = (bf16[416,256]{1,0:T(8,128)(2,1)S(1)}, bf16[416,256]{1,0:T(8,128)(2,1)S(1)}, u32[]{:S(2)}, u32[]{:S(2)}) collective-permute-start(bf16[416,256]{1,0:T(8,128)(2,1)S(1)} %collective-permute-done.9.refs_6_), channel_id=1, source_target_pairs={{0,4},{4,0},{8,12},{12,8},{16,20},{20,16},{24,28},{28,24},{32,36},... | collective-permute-start | bytes 638984 | tf_op jit(solution)/shard_map/ppermute | solution.py:265
  96.5 0.9 collective-permute-done.10.refs_7_
  97.4 8.2 %shard_map.162 = bf16[4,272,256]{2,1,0:T(8,128)(2,1)} custom-call(s32[4]{0:T(128)S(1)} %copy-done.12, bf16[256,256]{1,0:T(8,128)(2,1)S(1)} %bitcast.42, bf16[256,256]{1,0:T(8,128)(2,1)S(1)} %collective-permute-done.5.refs_1_, bf16[256,256]{1,0:T(8,128)(2,1)S(1)} %collective-permute-done.6.refs_2_, bf16[256,256]{1,0:T(8,128)(2,1)S(1)} %collective-permute-done.7.refs_3_, ...), custom_call_target="tpu_custom_call" | custom-call | tf_op jit(solution)/shard_map/pallas_call | solution.py:244
  105.6 3.6 %all-to-all-start.2 = ((bf16[4,272,256]{2,1,0:T(8,128)(2,1)}), bf16[4,272,256]{2,1,0:T(8,128)(2,1)S(1)}, u32[]{:S(2)}, u32[]{:S(2)}) async-start(bf16[4,272,256]{2,1,0:T(8,128)(2,1)} %shard_map.162), calls=%async_computation.2 | async-start | bytes 1114112 | tf_op jit(solution)/shard_map/all_to_all | solution.py:412
  109.3 0.7 copy-done.9
  109.9 5.9 %shard_map.164 = f32[256,512]{1,0:T(8,128)} custom-call(f32[256,512]{1,0:T(8,128)S(1)} %bitcast.32, bf16[256,512]{1,0:T(8,128)(2,1)S(1)} %bitcast.30, bf16[256,512]{1,0:T(8,128)(2,1)S(1)} %bitcast.38, f32[32,256]{1,0:T(8,128)S(1)} %add.74.bc_ref, f32[16,512]{1,0:T(8,128)S(1)} %bitcast.37, f32[1,512]{1,0:T(1,128)S(1)} %bitcast.44, ...), custom_call_target="tpu_custom_call" | custom-call | tf_op jit(solution)/shard_map/pallas_call | solution.py:244
  115.8 3.0 %all-to-all-done.2.part_ref = bf16[4,272,256]{2,1,0:T(8,128)(2,1)S(1)} async-done(((bf16[4,272,256]{2,1,0:T(8,128)(2,1)}), bf16[4,272,256]{2,1,0:T(8,128)(2,1)S(1)}, u32[]{:S(2)}, u32[]{:S(2)}) %all-to-all-start.2) | async-done | bytes 557088 | tf_op jit(solution)/shard_map/all_to_all | solution.py:412
  118.8 1.3 %shard_map.163 = f32[256,256]{1,0:T(8,128)} custom-call(bf16[4,272,256]{2,1,0:T(8,128)(2,1)S(1)} %all-to-all-done.2.part_ref), custom_call_target="tpu_custom_call" | custom-call | tf_op jit(solution)/shard_map/pallas_call | solution.py:244
  (53 shorter events, 1.1 us)
Async XLA Ops:
  0.6 0.8 copy-start
  0.6 20.6 %copy-start.3 = (bf16[16,16,8,256]{3,2,1,0:T(8,128)(2,1)S(1)}, bf16[16,16,8,256]{3,2,1,0:T(8,128)(2,1)}, u32[]{:S(2)}) copy-start(bf16[16,16,8,256]{3,2,1,0:T(8,128)(2,1)} %param.17) | copy-start | bytes 3145732
  3.3 28.9 %all-to-all-start = ((bf16[16,32,256]{2,1,0:T(8,128)(2,1)}), bf16[16,32,256]{2,1,0:T(8,128)(2,1)S(1)}, u32[]{:S(2)}, u32[]{:S(2)}) async-start(bf16[16,32,256]{2,1,0:T(8,128)(2,1)} %broadcast_in_dim.32), calls=%async_computation | async-start | bytes 524288 | tf_op jit(solution)/shard_map/all_to_all | solution.py:311
  22.9 37.8 %copy-start.4 = (bf16[1,256,8,256]{3,2,1,0:T(8,128)(2,1)S(1)}, bf16[1,256,8,256]{3,2,1,0:T(8,128)(2,1)}, u32[]{:S(2)}) copy-start(bf16[1,256,8,256]{3,2,1,0:T(8,128)(2,1)} %param.16) | copy-start | bytes 3145732
  32.2 51.0 %all-to-all-start.1 = ((bf16[128,8,256]{2,1,0:T(8,128)(2,1)}), bf16[128,8,256]{2,1,0:T(8,128)(2,1)S(1)}, u32[]{:S(2)}, u32[]{:S(2)}) async-start(bf16[128,8,256]{2,1,0:T(8,128)(2,1)} %bitcast.3), calls=%async_computation.1 | async-start | bytes 1048576 | tf_op jit(solution)/shard_map/all_to_all | solution.py:325
  47.9 12.8 %copy-start.8 = (f32[4,512,16]{1,2,0:T(8,128)S(1)}, f32[4,512,16]{1,2,0:T(8,128)}, u32[]{:S(2)}) copy-start(f32[4,512,16]{1,2,0:T(8,128)} %param.27) | copy-start | bytes 393220
  48.0 3.2 %copy-start.7 = (bf16[1,256,256]{2,1,0:T(8,128)(2,1)S(1)}, bf16[1,256,256]{2,1,0:T(8,128)(2,1)}, u32[]{:S(2)}) copy-start(bf16[1,256,256]{2,1,0:T(8,128)(2,1)} %param.15) | copy-start | bytes 393220
  48.0 17.1 %collective-permute-start = (f32[32,256]{1,0:T(8,128)S(1)}, f32[32,256]{1,0:T(8,128)S(1)}, u32[]{:S(2)}, u32[]{:S(2)}) collective-permute-start(f32[32,256]{1,0:T(8,128)S(1)} %convert_reduce_fusion), channel_id=1, source_target_pairs={{0,4},{4,0},{8,12},{12,8},{16,20},{20,16},{24,28},{28,24},{32,36},... | collective-permute-start | bytes 98312 | tf_op jit(solution)/shard_map/ppermute | solution.py:265
  51.1 29.2 %collective-permute-start.7 = (bf16[256,256]{1,0:T(8,128)(2,1)S(1)}, bf16[256,256]{1,0:T(8,128)(2,1)S(1)}, u32[]{:S(2)}, u32[]{:S(2)}) collective-permute-start(bf16[256,256]{1,0:T(8,128)(2,1)S(1)} %bitcast.39), channel_id=1, source_target_pairs={{0,384},{128,0},{256,128},{384,256},{1,385},{129,1},{257,129},{385... | collective-permute-start | bytes 393224 | tf_op jit(solution)/shard_map/ppermute | solution.py:256
  55.8 24.6 %collective-permute-start.6 = (bf16[256,256]{1,0:T(8,128)(2,1)S(1)}, bf16[256,256]{1,0:T(8,128)(2,1)S(1)}, u32[]{:S(2)}, u32[]{:S(2)}) collective-permute-start(bf16[256,256]{1,0:T(8,128)(2,1)S(1)} %bitcast.40), channel_id=1, source_target_pairs={{0,256},{128,384},{256,0},{384,128},{1,257},{129,385},{257,1},{385... | collective-permute-start | bytes 393224 | tf_op jit(solution)/shard_map/ppermute | solution.py:256
  58.1 22.3 %collective-permute-start.5 = (bf16[256,256]{1,0:T(8,128)(2,1)S(1)}, bf16[256,256]{1,0:T(8,128)(2,1)S(1)}, u32[]{:S(2)}, u32[]{:S(2)}) collective-permute-start(bf16[256,256]{1,0:T(8,128)(2,1)S(1)} %bitcast.41), channel_id=1, source_target_pairs={{0,128},{128,256},{256,384},{384,0},{1,129},{129,257},{257,385},{3... | collective-permute-start | bytes 393224 | tf_op jit(solution)/shard_map/ppermute | solution.py:256
  60.7 0.7 copy-start.10
  60.7 0.7 copy-start.11
  61.3 3.7 %copy-start.1 = (bf16[1,256,512]{2,1,0:T(8,128)(2,1)S(1)}, bf16[1,256,512]{2,1,0:T(8,128)(2,1)}, u32[]{:S(2)}) copy-start(bf16[1,256,512]{2,1,0:T(8,128)(2,1)} %param.21) | copy-start | bytes 786436
  61.3 3.7 %copy-start.2 = (f32[1,256,512]{2,1,0:T(8,128)S(1)}, f32[1,256,512]{2,1,0:T(8,128)}, u32[]{:S(2)}) copy-start(f32[1,256,512]{2,1,0:T(8,128)} %param.23) | copy-start | bytes 1572868
  62.2 2.9 %copy-start.5 = (f32[512,16]{0,1:T(8,128)S(1)}, f32[512,16]{0,1:T(8,128)}, u32[]{:S(2)}) copy-start(f32[512,16]{0,1:T(8,128)} %param.25) | copy-start | bytes 98308
  62.2 9.8 %collective-permute-start.3 = (f32[2,16,512]{2,1,0:T(8,128)S(1)}, f32[2,16,512]{2,1,0:T(8,128)S(1)}, u32[]{:S(2)}, u32[]{:S(2)}) collective-permute-start(f32[2,16,512]{2,1,0:T(8,128)S(1)} %get-tuple-element.32), channel_id=1, source_target_pairs={{0,1},{1,0},{2,3},{3,2},{4,5},{5,4},{6,7},{7,6},{8,9},{9,8},{10,11... | collective-permute-start | bytes 196616 | tf_op jit(solution)/shard_map/ppermute | solution.py:349
  68.5 8.3 %collective-permute-start.1 = (f32[24,512]{1,0:T(8,128)S(1)}, f32[24,512]{1,0:T(8,128)S(1)}, u32[]{:S(2)}, u32[]{:S(2)}) collective-permute-start(f32[24,512]{1,0:T(8,128)S(1)} %shard_map.159), channel_id=1, source_target_pairs={{0,128},{128,256},{256,384},{384,0},{1,129},{129,257},{257,385},{3... | collective-permute-start | bytes 147464 | tf_op jit(solution)/shard_map/ppermute | solution.py:256
  72.0 8.3 %collective-permute-start.4 = (f32[16,512]{1,0:T(8,128)S(1)}, f32[16,512]{1,0:T(8,128)S(1)}, u32[]{:S(2)}, u32[]{:S(2)}) collective-permute-start(f32[16,512]{1,0:T(8,128)S(1)} %fusion), channel_id=1, source_target_pairs={{0,2},{1,3},{2,0},{3,1},{4,6},{5,7},{6,4},{7,5},{8,10},{9,11},{10,... | collective-permute-start | bytes 98312 | tf_op jit(solution)/shard_map/ppermute | solution.py:353
  76.8 6.3 %collective-permute-start.2 = (f32[24,512]{1,0:T(8,128)S(1)}, f32[24,512]{1,0:T(8,128)S(1)}, u32[]{:S(2)}, u32[]{:S(2)}) collective-permute-start(f32[24,512]{1,0:T(8,128)S(1)} %maximum_select_fusion), channel_id=1, source_target_pairs={{0,256},{128,384},{256,0},{384,128},{1,257},{129,385},{257,1},{385... | collective-permute-start | bytes 147464 | tf_op jit(solution)/shard_map/ppermute | solution.py:256
  83.2 14.2 %copy-start.12 = (s32[4]{0:T(128)S(1)}, s32[4]{0:T(128)}, u32[]{:S(2)}) copy-start(s32[4]{0:T(128)} %prefix_ref.1) | copy-start | bytes 52
  83.7 8.3 %collective-permute-start.9 = (bf16[416,256]{1,0:T(8,128)(2,1)S(1)}, bf16[416,256]{1,0:T(8,128)(2,1)S(1)}, u32[]{:S(2)}, u32[]{:S(2)}) collective-permute-start(bf16[416,256]{1,0:T(8,128)(2,1)S(1)} %shard_map.161.refs_4_), channel_id=1, source_target_pairs={{0,8},{4,12},{8,0},{12,4},{16,24},{20,28},{24,16},{28,20},{32,40},... | collective-permute-start | bytes 638984 | tf_op jit(solution)/shard_map/ppermute | solution.py:265
  86.8 9.7 %collective-permute-start.8 = (bf16[416,256]{1,0:T(8,128)(2,1)S(1)}, bf16[416,256]{1,0:T(8,128)(2,1)S(1)}, u32[]{:S(2)}, u32[]{:S(2)}) collective-permute-start(bf16[416,256]{1,0:T(8,128)(2,1)S(1)} %shard_map.161.refs_4_), channel_id=1, source_target_pairs={{0,4},{4,0},{8,12},{12,8},{16,20},{20,16},{24,28},{28,24},{32,36},... | collective-permute-start | bytes 638984 | tf_op jit(solution)/shard_map/ppermute | solution.py:265
  92.0 5.4 %collective-permute-start.10 = (bf16[416,256]{1,0:T(8,128)(2,1)S(1)}, bf16[416,256]{1,0:T(8,128)(2,1)S(1)}, u32[]{:S(2)}, u32[]{:S(2)}) collective-permute-start(bf16[416,256]{1,0:T(8,128)(2,1)S(1)} %collective-permute-done.9.refs_6_), channel_id=1, source_target_pairs={{0,4},{4,0},{8,12},{12,8},{16,20},{20,16},{24,28},{28,24},{32,36},... | collective-permute-start | bytes 638984 | tf_op jit(solution)/shard_map/ppermute | solution.py:265
  105.6 3.6 %copy-start.6 = (bf16[1,256,512]{2,1,0:T(8,128)(2,1)S(1)}, bf16[1,256,512]{2,1,0:T(8,128)(2,1)}, u32[]{:S(2)}) copy-start(bf16[1,256,512]{2,1,0:T(8,128)(2,1)} %param.22) | copy-start | bytes 786436
  105.6 13.2 %all-to-all-start.2 = ((bf16[4,272,256]{2,1,0:T(8,128)(2,1)}), bf16[4,272,256]{2,1,0:T(8,128)(2,1)S(1)}, u32[]{:S(2)}, u32[]{:S(2)}) async-start(bf16[4,272,256]{2,1,0:T(8,128)(2,1)} %shard_map.162), calls=%async_computation.2 | async-start | bytes 1114112 | tf_op jit(solution)/shard_map/all_to_all | solution.py:412
  109.2 0.7 copy-start.9

commit v4 on v3

--- a/solution.py
+++ b/solution.py
@@ -50,6 +50,17 @@
     out_ref[...] = jnp.dot(pick, received_ref[...], preferred_element_type=jnp.float32).astype(
         jnp.bfloat16
     )
+
+
+def project_kernel(weight_ref, input_ref, out_ref):
+    sums = lax.dot_general(
+        weight_ref[...],
+        input_ref[...],
+        (((1,), (1,)), ((), ())),
+        preferred_element_type=jnp.float32,
+    ).astype(jnp.bfloat16)
+    for chip in range(out_ref.shape[0]):
+        out_ref[chip] = sums
 
 
 def prepare_kernel(owner_ref, slot_ref, state_ref, span_ref, pair_ref, crossing_ref, near_ref, tile_ref):
@@ -302,10 +313,13 @@
     chosen = jnp.sum(jnp.where(hit, quarter_slot[:, None, :], 0), axis=2).reshape(-1)
 
     inputs = ssm_input[0]
-    sums = lax.dot_general(
-        bc_weight, inputs, (((0,), (1,)), ((), ())), preferred_element_type=jnp.float32
-    )
-    sums = jnp.broadcast_to(sums.astype(jnp.bfloat16)[None], (n_mp // 2,) + sums.shape)
+    sums = call(
+        project_kernel,
+        jax.ShapeDtypeStruct((n_mp // 2, bc_weight.shape[1], tok_rows), jnp.bfloat16),
+        [vmem()] * 2,
+        (bc_weight.T, inputs),
+        24,
+    )
     sums, pool_kv = lax.optimization_barrier((sums, pool_kv))
     chips = [[2 * chip + core for chip in range(n_mp // 2)] for core in range(2)]
     sums = lax.all_to_all(

time: 121 us -> 121 us (level)
    pallas_call x6 -> x7, Pallas kernels: 20.9 us -> 22 us  [call(): pl.pallas_call(kernel, out_shape=out, in_specs=specs, out_specs=vmem(), s...]
    unnamed x26 -> x30, local copies, waits for them, and re-layouts: 2.09 us -> 3.06 us
where the time goes in v4:
time: 121 us; the launch traced here: 120 us
  starting transfers between devices  74.8 us (62%)
  Pallas kernels  22.8 us (19%)
  waiting for transfers between devices  16.6 us (14%)
  local copies, waits for them, and re-layouts  4.26 us (4%)
    pallas_call x7, Pallas kernels, call(): pl.pallas_call(kernel, out_shape=out, in_specs=specs, out_specs=vmem(), s...  22 us
    ppermute x5, starting transfers between devices, shifted(): lax.ppermute(value, axis, [(i, (i + steps) % count) for i in range(count)])  16.5 us
    all_to_all x1, starting transfers between devices, on_device(): lax.all_to_all(sums, 'mp', split_axis=0, concat_axis=0, tiled=True, axis_...  15.7 us
    ppermute x4, starting transfers between devices, swapped(): lax.ppermute(value, 'mp', [(source, source ^ flip) for source in range(co...  15.7 us
    all_to_all x1, starting transfers between devices, on_device(): lax.all_to_all(outgoing.reshape(n_cache * n_mp, 2 * page_part, width), ('...  15.7 us
    all_to_all x1, waiting for transfers between devices, on_device(): lax.all_to_all(sums, 'mp', split_axis=0, concat_axis=0, tiled=True, axis_...  9.94 us
    ppermute x1, starting transfers between devices, on_device(): lax.ppermute(crossing, 'cache', [(i, i ^ 2) for i in range(n_cache)])  4.74 us
    all_to_all x1, starting transfers between devices, on_device(): lax.all_to_all(partial, 'seq', split_axis=0, concat_axis=0, tiled=True)  3.6 us
  transfers between devices with their start and end apart: 14, of which 4 were waited for; matrix products, arithmetic and copies ran while one was open for 2% of the time, Pallas kernels for 10%

profile of v4, /device:TPU:1, one launch (start us, length us, event | category | flops | bytes accessed | tf_op | source)
XLA Modules:
  0.0 120.2 jit_solution(1130754504284585228)
XLA Ops:
  0.7 0.9 copy-done.1
  1.6 0.8 copy-done.10
  2.4 0.9 shard_map.158
  3.3 15.7 %all-to-all-start = ((bf16[16,32,256]{2,1,0:T(8,128)(2,1)}), bf16[16,32,256]{2,1,0:T(8,128)(2,1)S(1)}, u32[]{:S(2)}, u32[]{:S(2)}) async-start(bf16[16,32,256]{2,1,0:T(8,128)(2,1)} %shard_map.158), calls=%async_computation | async-start | bytes 524288 | tf_op jit(solution)/shard_map/all_to_all | solution.py:325
  19.1 0.8 constant_dynamic-slice_fusion
  20.0 0.2 convert_reduce_fusion.1
  20.6 1.7 %shard_map.159 = bf16[4,256,256]{2,1,0:T(8,128)(2,1)} custom-call(s32[8]{0:T(128)S(1)} %reshape.79.chosen_ref, bf16[16,128,256]{2,1,0:T(8,128)(2,1)S(1)} %bitcast.33), custom_call_target="tpu_custom_call" | custom-call | tf_op jit(solution)/shard_map/pallas_call | solution.py:255
  22.2 9.9 %all-to-all-done = bf16[16,32,256]{2,1,0:T(8,128)(2,1)S(1)} async-done(((bf16[16,32,256]{2,1,0:T(8,128)(2,1)}), bf16[16,32,256]{2,1,0:T(8,128)(2,1)S(1)}, u32[]{:S(2)}, u32[]{:S(2)}) %all-to-all-start) | async-done | bytes 262176 | tf_op jit(solution)/shard_map/all_to_all | solution.py:325
  32.2 15.7 %all-to-all-start.1 = ((bf16[128,8,256]{2,1,0:T(8,128)(2,1)}), bf16[128,8,256]{2,1,0:T(8,128)(2,1)S(1)}, u32[]{:S(2)}, u32[]{:S(2)}) async-start(bf16[128,8,256]{2,1,0:T(8,128)(2,1)} %bitcast.4), calls=%async_computation.1 | async-start | bytes 1048576 | tf_op jit(solution)/shard_map/all_to_all | solution.py:339
  48.0 2.9 %collective-permute-start = (f32[32,256]{1,0:T(8,128)S(1)}, f32[32,256]{1,0:T(8,128)S(1)}, u32[]{:S(2)}, u32[]{:S(2)}) collective-permute-start(f32[32,256]{1,0:T(8,128)S(1)} %convert_reduce_fusion), channel_id=1, source_target_pairs={{0,4},{4,0},{8,12},{12,8},{16,20},{20,16},{24,28},{28,24},{32,36},... | collective-permute-start | bytes 98312 | tf_op jit(solution)/shard_map/ppermute | solution.py:276
  51.2 4.6 %collective-permute-start.7 = (bf16[256,256]{1,0:T(8,128)(2,1)S(1)}, bf16[256,256]{1,0:T(8,128)(2,1)S(1)}, u32[]{:S(2)}, u32[]{:S(2)}) collective-permute-start(bf16[256,256]{1,0:T(8,128)(2,1)S(1)} %bitcast.38), channel_id=1, source_target_pairs={{0,384},{128,0},{256,128},{384,256},{1,385},{129,1},{257,129},{385... | collective-permute-start | bytes 393224 | tf_op jit(solution)/shard_map/ppermute | solution.py:267
  55.8 2.3 %collective-permute-start.6 = (bf16[256,256]{1,0:T(8,128)(2,1)S(1)}, bf16[256,256]{1,0:T(8,128)(2,1)S(1)}, u32[]{:S(2)}, u32[]{:S(2)}) collective-permute-start(bf16[256,256]{1,0:T(8,128)(2,1)S(1)} %bitcast.39), channel_id=1, source_target_pairs={{0,256},{128,384},{256,0},{384,128},{1,257},{129,385},{257,1},{385... | collective-permute-start | bytes 393224 | tf_op jit(solution)/shard_map/ppermute | solution.py:267
  58.1 2.6 %collective-permute-start.5 = (bf16[256,256]{1,0:T(8,128)(2,1)S(1)}, bf16[256,256]{1,0:T(8,128)(2,1)S(1)}, u32[]{:S(2)}, u32[]{:S(2)}) collective-permute-start(bf16[256,256]{1,0:T(8,128)(2,1)S(1)} %bitcast.40), channel_id=1, source_target_pairs={{0,128},{128,256},{256,384},{384,0},{1,129},{129,257},{257,385},{3... | collective-permute-start | bytes 393224 | tf_op jit(solution)/shard_map/ppermute | solution.py:267
  60.7 0.6 copy-done.12
  61.4 0.8 shard_map.161
  62.2 2.9 %collective-permute-start.3 = (f32[2,16,512]{2,1,0:T(8,128)S(1)}, f32[2,16,512]{2,1,0:T(8,128)S(1)}, u32[]{:S(2)}, u32[]{:S(2)}) collective-permute-start(f32[2,16,512]{2,1,0:T(8,128)S(1)} %get-tuple-element.32), channel_id=1, source_target_pairs={{0,1},{1,0},{2,3},{3,2},{4,5},{5,4},{6,7},{7,6},{8,9},{9,8},{10,11... | collective-permute-start | bytes 196616 | tf_op jit(solution)/shard_map/ppermute | solution.py:363
  65.1 3.4 %shard_map.160 = f32[24,512]{1,0:T(8,128)S(1)} custom-call(f32[256,512]{1,0:T(8,128)S(1)} %bitcast.30, bf16[256,512]{1,0:T(8,128)(2,1)S(1)} %bitcast.28, f32[32,256]{1,0:T(8,128)S(1)} %add.74.bc_ref, f32[16,512]{1,0:T(8,128)S(1)} %bitcast.35), custom_call_target="tpu_custom_call" | custom-call | tf_op jit(solution)/shard_map/pallas_call | solution.py:255
  68.5 3.5 %collective-permute-start.1 = (f32[24,512]{1,0:T(8,128)S(1)}, f32[24,512]{1,0:T(8,128)S(1)}, u32[]{:S(2)}, u32[]{:S(2)}) collective-permute-start(f32[24,512]{1,0:T(8,128)S(1)} %shard_map.160), channel_id=1, source_target_pairs={{0,128},{128,256},{256,384},{384,0},{1,129},{129,257},{257,385},{3... | collective-permute-start | bytes 147464 | tf_op jit(solution)/shard_map/ppermute | solution.py:267
  72.0 4.7 %collective-permute-start.4 = (f32[16,512]{1,0:T(8,128)S(1)}, f32[16,512]{1,0:T(8,128)S(1)}, u32[]{:S(2)}, u32[]{:S(2)}) collective-permute-start(f32[16,512]{1,0:T(8,128)S(1)} %fusion), channel_id=1, source_target_pairs={{0,2},{1,3},{2,0},{3,1},{4,6},{5,7},{6,4},{7,5},{8,10},{9,11},{10,... | collective-permute-start | bytes 98312 | tf_op jit(solution)/shard_map/ppermute | solution.py:367
  76.9 3.5 %collective-permute-start.2 = (f32[24,512]{1,0:T(8,128)S(1)}, f32[24,512]{1,0:T(8,128)S(1)}, u32[]{:S(2)}, u32[]{:S(2)}) collective-permute-start(f32[24,512]{1,0:T(8,128)S(1)} %maximum_select_fusion), channel_id=1, source_target_pairs={{0,256},{128,384},{256,0},{384,128},{1,257},{129,385},{257,1},{385... | collective-permute-start | bytes 147464 | tf_op jit(solution)/shard_map/ppermute | solution.py:267
  80.4 2.8 %collective-permute-done.2.rest_1_ = f32[24,512]{1,0:T(8,128)S(1)} collective-permute-done((f32[24,512]{1,0:T(8,128)S(1)}, f32[24,512]{1,0:T(8,128)S(1)}, u32[]{:S(2)}, u32[]{:S(2)}) %collective-permute-start.2) | collective-permute-done | bytes 49184 | tf_op jit(solution)/shard_map/ppermute | solution.py:267
  83.2 0.5 shard_map.162.refs_4_
  83.7 3.1 %collective-permute-start.9 = (bf16[416,256]{1,0:T(8,128)(2,1)S(1)}, bf16[416,256]{1,0:T(8,128)(2,1)S(1)}, u32[]{:S(2)}, u32[]{:S(2)}) collective-permute-start(bf16[416,256]{1,0:T(8,128)(2,1)S(1)} %shard_map.162.refs_4_), channel_id=1, source_target_pairs={{0,8},{4,12},{8,0},{12,4},{16,24},{20,28},{24,16},{28,20},{32,40},... | collective-permute-start | bytes 638984 | tf_op jit(solution)/shard_map/ppermute | solution.py:276
  86.9 5.2 %collective-permute-start.8 = (bf16[416,256]{1,0:T(8,128)(2,1)S(1)}, bf16[416,256]{1,0:T(8,128)(2,1)S(1)}, u32[]{:S(2)}, u32[]{:S(2)}) collective-permute-start(bf16[416,256]{1,0:T(8,128)(2,1)S(1)} %shard_map.162.refs_4_), channel_id=1, source_target_pairs={{0,4},{4,0},{8,12},{12,8},{16,20},{20,16},{24,28},{28,24},{32,36},... | collective-permute-start | bytes 638984 | tf_op jit(solution)/shard_map/ppermute | solution.py:276
  92.1 4.5 %collective-permute-start.10 = (bf16[416,256]{1,0:T(8,128)(2,1)S(1)}, bf16[416,256]{1,0:T(8,128)(2,1)S(1)}, u32[]{:S(2)}, u32[]{:S(2)}) collective-permute-start(bf16[416,256]{1,0:T(8,128)(2,1)S(1)} %collective-permute-done.9.refs_6_), channel_id=1, source_target_pairs={{0,4},{4,0},{8,12},{12,8},{16,20},{20,16},{24,28},{28,24},{32,36},... | collective-permute-start | bytes 638984 | tf_op jit(solution)/shard_map/ppermute | solution.py:276
  96.6 0.9 collective-permute-done.10.refs_7_
  97.4 8.4 %shard_map.163 = bf16[4,272,256]{2,1,0:T(8,128)(2,1)} custom-call(s32[4]{0:T(128)S(1)} %copy-done.14, bf16[256,256]{1,0:T(8,128)(2,1)S(1)} %bitcast.41, bf16[256,256]{1,0:T(8,128)(2,1)S(1)} %collective-permute-done.5.refs_1_, bf16[256,256]{1,0:T(8,128)(2,1)S(1)} %collective-permute-done.6.refs_2_, bf16[256,256]{1,0:T(8,128)(2,1)S(1)} %collective-permute-done.7.refs_3_, ...), custom_call_target="tpu_custom_call" | custom-call | tf_op jit(solution)/shard_map/pallas_call | solution.py:255
  105.8 3.6 %all-to-all-start.2 = ((bf16[4,272,256]{2,1,0:T(8,128)(2,1)}), bf16[4,272,256]{2,1,0:T(8,128)(2,1)S(1)}, u32[]{:S(2)}, u32[]{:S(2)}) async-start(bf16[4,272,256]{2,1,0:T(8,128)(2,1)} %shard_map.163), calls=%async_computation.2 | async-start | bytes 1114112 | tf_op jit(solution)/shard_map/all_to_all | solution.py:426
  109.5 0.7 copy-done.11
  110.1 5.9 %shard_map.165 = f32[256,512]{1,0:T(8,128)} custom-call(f32[256,512]{1,0:T(8,128)S(1)} %bitcast.31, bf16[256,512]{1,0:T(8,128)(2,1)S(1)} %bitcast.29, bf16[256,512]{1,0:T(8,128)(2,1)S(1)} %bitcast.37, f32[32,256]{1,0:T(8,128)S(1)} %add.74.bc_ref, f32[16,512]{1,0:T(8,128)S(1)} %bitcast.36, f32[1,512]{1,0:T(1,128)S(1)} %bitcast.44, ...), custom_call_target="tpu_custom_call" | custom-call | tf_op jit(solution)/shard_map/pallas_call | solution.py:255
  116.0 3.0 %all-to-all-done.2.part_ref = bf16[4,272,256]{2,1,0:T(8,128)(2,1)S(1)} async-done(((bf16[4,272,256]{2,1,0:T(8,128)(2,1)}), bf16[4,272,256]{2,1,0:T(8,128)(2,1)S(1)}, u32[]{:S(2)}, u32[]{:S(2)}) %all-to-all-start.2) | async-done | bytes 557088 | tf_op jit(solution)/shard_map/all_to_all | solution.py:426
  119.0 1.3 %shard_map.164 = f32[256,256]{1,0:T(8,128)} custom-call(bf16[4,272,256]{2,1,0:T(8,128)(2,1)S(1)} %all-to-all-done.2.part_ref), custom_call_target="tpu_custom_call" | custom-call | tf_op jit(solution)/shard_map/pallas_call | solution.py:255
  (56 shorter events, 1.0 us)
Async XLA Ops:
  0.6 18.4 %copy-start = (s32[4,416,1]{1,2,0:T(1,128)S(1)}, s32[4,416,1]{1,2,0:T(1,128)}, u32[]{:S(2)}) copy-start(s32[4,416,1]{1,2,0:T(1,128)} %param.18) | copy-start | bytes 19972
  0.6 1.0 copy-start.1
  1.6 0.8 copy-start.10
  2.4 18.2 %copy-start.4 = (bf16[16,16,8,256]{3,2,1,0:T(8,128)(2,1)S(1)}, bf16[16,16,8,256]{3,2,1,0:T(8,128)(2,1)}, u32[]{:S(2)}) copy-start(bf16[16,16,8,256]{3,2,1,0:T(8,128)(2,1)} %param.17) | copy-start | bytes 3145732
  3.3 28.9 %all-to-all-start = ((bf16[16,32,256]{2,1,0:T(8,128)(2,1)}), bf16[16,32,256]{2,1,0:T(8,128)(2,1)S(1)}, u32[]{:S(2)}, u32[]{:S(2)}) async-start(bf16[16,32,256]{2,1,0:T(8,128)(2,1)} %shard_map.158), calls=%async_computation | async-start | bytes 524288 | tf_op jit(solution)/shard_map/all_to_all | solution.py:325
  22.2 38.5 %copy-start.5 = (bf16[1,256,8,256]{3,2,1,0:T(8,128)(2,1)S(1)}, bf16[1,256,8,256]{3,2,1,0:T(8,128)(2,1)}, u32[]{:S(2)}) copy-start(bf16[1,256,8,256]{3,2,1,0:T(8,128)(2,1)} %param.16) | copy-start | bytes 3145732
  32.2 51.0 %all-to-all-start.1 = ((bf16[128,8,256]{2,1,0:T(8,128)(2,1)}), bf16[128,8,256]{2,1,0:T(8,128)(2,1)S(1)}, u32[]{:S(2)}, u32[]{:S(2)}) async-start(bf16[128,8,256]{2,1,0:T(8,128)(2,1)} %bitcast.4), calls=%async_computation.1 | async-start | bytes 1048576 | tf_op jit(solution)/shard_map/all_to_all | solution.py:339
  47.9 12.8 %copy-start.9 = (f32[4,512,16]{1,2,0:T(8,128)S(1)}, f32[4,512,16]{1,2,0:T(8,128)}, u32[]{:S(2)}) copy-start(f32[4,512,16]{1,2,0:T(8,128)} %param.27) | copy-start | bytes 393220
  48.0 3.2 %copy-start.8 = (bf16[1,256,256]{2,1,0:T(8,128)(2,1)S(1)}, bf16[1,256,256]{2,1,0:T(8,128)(2,1)}, u32[]{:S(2)}) copy-start(bf16[1,256,256]{2,1,0:T(8,128)(2,1)} %param.15) | copy-start | bytes 393220
  48.0 17.1 %collective-permute-start = (f32[32,256]{1,0:T(8,128)S(1)}, f32[32,256]{1,0:T(8,128)S(1)}, u32[]{:S(2)}, u32[]{:S(2)}) collective-permute-start(f32[32,256]{1,0:T(8,128)S(1)} %convert_reduce_fusion), channel_id=1, source_target_pairs={{0,4},{4,0},{8,12},{12,8},{16,20},{20,16},{24,28},{28,24},{32,36},... | collective-permute-start | bytes 98312 | tf_op jit(solution)/shard_map/ppermute | solution.py:276
  51.2 29.2 %collective-permute-start.7 = (bf16[256,256]{1,0:T(8,128)(2,1)S(1)}, bf16[256,256]{1,0:T(8,128)(2,1)S(1)}, u32[]{:S(2)}, u32[]{:S(2)}) collective-permute-start(bf16[256,256]{1,0:T(8,128)(2,1)S(1)} %bitcast.38), channel_id=1, source_target_pairs={{0,384},{128,0},{256,128},{384,256},{1,385},{129,1},{257,129},{385... | collective-permute-start | bytes 393224 | tf_op jit(solution)/shard_map/ppermute | solution.py:267
  55.8 24.6 %collective-permute-start.6 = (bf16[256,256]{1,0:T(8,128)(2,1)S(1)}, bf16[256,256]{1,0:T(8,128)(2,1)S(1)}, u32[]{:S(2)}, u32[]{:S(2)}) collective-permute-start(bf16[256,256]{1,0:T(8,128)(2,1)S(1)} %bitcast.39), channel_id=1, source_target_pairs={{0,256},{128,384},{256,0},{384,128},{1,257},{129,385},{257,1},{385... | collective-permute-start | bytes 393224 | tf_op jit(solution)/shard_map/ppermute | solution.py:267
  58.1 22.3 %collective-permute-start.5 = (bf16[256,256]{1,0:T(8,128)(2,1)S(1)}, bf16[256,256]{1,0:T(8,128)(2,1)S(1)}, u32[]{:S(2)}, u32[]{:S(2)}) collective-permute-start(bf16[256,256]{1,0:T(8,128)(2,1)S(1)} %bitcast.40), channel_id=1, source_target_pairs={{0,128},{128,256},{256,384},{384,0},{1,129},{129,257},{257,385},{3... | collective-permute-start | bytes 393224 | tf_op jit(solution)/shard_map/ppermute | solution.py:267
  60.7 0.7 copy-start.12
  60.7 0.7 copy-start.13
  61.4 3.7 %copy-start.2 = (bf16[1,256,512]{2,1,0:T(8,128)(2,1)S(1)}, bf16[1,256,512]{2,1,0:T(8,128)(2,1)}, u32[]{:S(2)}) copy-start(bf16[1,256,512]{2,1,0:T(8,128)(2,1)} %param.21) | copy-start | bytes 786436
  61.4 3.7 %copy-start.3 = (f32[1,256,512]{2,1,0:T(8,128)S(1)}, f32[1,256,512]{2,1,0:T(8,128)}, u32[]{:S(2)}) copy-start(f32[1,256,512]{2,1,0:T(8,128)} %param.23) | copy-start | bytes 1572868
  62.2 2.9 %copy-start.6 = (f32[512,16]{0,1:T(8,128)S(1)}, f32[512,16]{0,1:T(8,128)}, u32[]{:S(2)}) copy-start(f32[512,16]{0,1:T(8,128)} %param.25) | copy-start | bytes 98308
  62.2 9.8 %collective-permute-start.3 = (f32[2,16,512]{2,1,0:T(8,128)S(1)}, f32[2,16,512]{2,1,0:T(8,128)S(1)}, u32[]{:S(2)}, u32[]{:S(2)}) collective-permute-start(f32[2,16,512]{2,1,0:T(8,128)S(1)} %get-tuple-element.32), channel_id=1, source_target_pairs={{0,1},{1,0},{2,3},{3,2},{4,5},{5,4},{6,7},{7,6},{8,9},{9,8},{10,11... | collective-permute-start | bytes 196616 | tf_op jit(solution)/shard_map/ppermute | solution.py:363
  68.5 8.3 %collective-permute-start.1 = (f32[24,512]{1,0:T(8,128)S(1)}, f32[24,512]{1,0:T(8,128)S(1)}, u32[]{:S(2)}, u32[]{:S(2)}) collective-permute-start(f32[24,512]{1,0:T(8,128)S(1)} %shard_map.160), channel_id=1, source_target_pairs={{0,128},{128,256},{256,384},{384,0},{1,129},{129,257},{257,385},{3... | collective-permute-start | bytes 147464 | tf_op jit(solution)/shard_map/ppermute | solution.py:267
  72.0 8.3 %collective-permute-start.4 = (f32[16,512]{1,0:T(8,128)S(1)}, f32[16,512]{1,0:T(8,128)S(1)}, u32[]{:S(2)}, u32[]{:S(2)}) collective-permute-start(f32[16,512]{1,0:T(8,128)S(1)} %fusion), channel_id=1, source_target_pairs={{0,2},{1,3},{2,0},{3,1},{4,6},{5,7},{6,4},{7,5},{8,10},{9,11},{10,... | collective-permute-start | bytes 98312 | tf_op jit(solution)/shard_map/ppermute | solution.py:367
  76.9 6.3 %collective-permute-start.2 = (f32[24,512]{1,0:T(8,128)S(1)}, f32[24,512]{1,0:T(8,128)S(1)}, u32[]{:S(2)}, u32[]{:S(2)}) collective-permute-start(f32[24,512]{1,0:T(8,128)S(1)} %maximum_select_fusion), channel_id=1, source_target_pairs={{0,256},{128,384},{256,0},{384,128},{1,257},{129,385},{257,1},{385... | collective-permute-start | bytes 147464 | tf_op jit(solution)/shard_map/ppermute | solution.py:267
  83.2 14.2 %copy-start.14 = (s32[4]{0:T(128)S(1)}, s32[4]{0:T(128)}, u32[]{:S(2)}) copy-start(s32[4]{0:T(128)} %prefix_ref.1) | copy-start | bytes 52
  83.7 8.3 %collective-permute-start.9 = (bf16[416,256]{1,0:T(8,128)(2,1)S(1)}, bf16[416,256]{1,0:T(8,128)(2,1)S(1)}, u32[]{:S(2)}, u32[]{:S(2)}) collective-permute-start(bf16[416,256]{1,0:T(8,128)(2,1)S(1)} %shard_map.162.refs_4_), channel_id=1, source_target_pairs={{0,8},{4,12},{8,0},{12,4},{16,24},{20,28},{24,16},{28,20},{32,40},... | collective-permute-start | bytes 638984 | tf_op jit(solution)/shard_map/ppermute | solution.py:276
  86.9 9.7 %collective-permute-start.8 = (bf16[416,256]{1,0:T(8,128)(2,1)S(1)}, bf16[416,256]{1,0:T(8,128)(2,1)S(1)}, u32[]{:S(2)}, u32[]{:S(2)}) collective-permute-start(bf16[416,256]{1,0:T(8,128)(2,1)S(1)} %shard_map.162.refs_4_), channel_id=1, source_target_pairs={{0,4},{4,0},{8,12},{12,8},{16,20},{20,16},{24,28},{28,24},{32,36},... | collective-permute-start | bytes 638984 | tf_op jit(solution)/shard_map/ppermute | solution.py:276
  92.1 5.4 %collective-permute-start.10 = (bf16[416,256]{1,0:T(8,128)(2,1)S(1)}, bf16[416,256]{1,0:T(8,128)(2,1)S(1)}, u32[]{:S(2)}, u32[]{:S(2)}) collective-permute-start(bf16[416,256]{1,0:T(8,128)(2,1)S(1)} %collective-permute-done.9.refs_6_), channel_id=1, source_target_pairs={{0,4},{4,0},{8,12},{12,8},{16,20},{20,16},{24,28},{28,24},{32,36},... | collective-permute-start | bytes 638984 | tf_op jit(solution)/shard_map/ppermute | solution.py:276
  105.8 3.6 %copy-start.7 = (bf16[1,256,512]{2,1,0:T(8,128)(2,1)S(1)}, bf16[1,256,512]{2,1,0:T(8,128)(2,1)}, u32[]{:S(2)}) copy-start(bf16[1,256,512]{2,1,0:T(8,128)(2,1)} %param.22) | copy-start | bytes 786436
  105.8 13.2 %all-to-all-start.2 = ((bf16[4,272,256]{2,1,0:T(8,128)(2,1)}), bf16[4,272,256]{2,1,0:T(8,128)(2,1)S(1)}, u32[]{:S(2)}, u32[]{:S(2)}) async-start(bf16[4,272,256]{2,1,0:T(8,128)(2,1)} %shard_map.163), calls=%async_computation.2 | async-start | bytes 1114112 | tf_op jit(solution)/shard_map/all_to_all | solution.py:426
  109.4 0.7 copy-start.11
